TPU v7x, 128 devices: a whole 4x4x4 slice. The times are simulated.
128 devices in a mesh: dp: 8 (over y, core), expert: 16 (over z, x).
Axes of the slice: x: 4, y: 4, z: 4, core: 2. Of those that a mesh axis runs over, the one named last changes fastest.
Arguments:
- tokens: bfloat16 [16384, 2048], P(('dp', 'expert')), may hold values from -6 to 6
- expert_ids: int32 [16384], P(('dp', 'expert')), may hold values from 0 to 31, as said below
- gate_weights: float32 [16384], P(('dp', 'expert')), may hold values from 0.25 to 1
- in_weights: bfloat16 [32, 2048, 4096], P('expert', None, 'dp'), may hold values from -0.125 to 0.125
- out_weights: bfloat16 [32, 4096, 2048], P('expert', 'dp'), may hold values from -0.09375 to 0.09375
- cotangent: bfloat16 [16384, 2048], P(('dp', 'expert')), may hold values from -6 to 6
Outputs:
- mixed: bfloat16 [16384, 2048], P(('dp', 'expert'))
- gate_grad: float32 [16384], P(('dp', 'expert'))
- token_grad: bfloat16 [16384, 2048], P(('dp', 'expert'))
- in_weights_grad: bfloat16 [32, 2048, 4096], P('expert', None, 'dp')
- out_weights_grad: bfloat16 [32, 4096, 2048], P('expert', 'dp')
Inputs may be any that keep to these rules, and one draw needn't show every extreme that they name: `expert_ids`: within each device's aligned block of 128 rows no expert is named more than 8 times, and one and the same expert is named exactly 8 times in every block; every expert is named somewhere.
All inputs are finite; a program needn't handle non-finite values.
Results may differ from a plain program's by a relative error of at most 0.015.
Values may be sent and summed in bfloat16 or wider, within the bound.
A program may use at most 192 MiB of HBM per device.

v0:
```python
import jax
import jax.numpy as jnp
from jax import lax
from jax.sharding import PartitionSpec as P

root_half = 0.7071067811865476
inv_root_tau = 0.3989422804014327


def gelu_value(values):
    return 0.5 * values * (1.0 + lax.erf(values * root_half))


def gelu_slope(values):
    return (
        0.5 * (1.0 + lax.erf(values * root_half))
        + values * jnp.exp(-0.5 * values * values) * inv_root_tau
    )


def dispatch(sent_x, sent_g, local_experts):
    dp_count = lax.axis_size("dp")
    ex_count = lax.axis_size("expert")
    capacity = sent_x.shape[1]
    features = sent_x.shape[2]
    copies_x = jnp.broadcast_to(sent_x[None], (dp_count,) + sent_x.shape).reshape(
        dp_count * ex_count, local_experts, capacity, features
    )
    copies_g = jnp.broadcast_to(sent_g[None], (dp_count,) + sent_g.shape).reshape(
        dp_count * ex_count, local_experts, capacity, features
    )
    routed_x, routed_g = (
        lax.all_to_all(copies_x, ("dp", "expert"), split_axis=0, concat_axis=0, tiled=True),
        lax.all_to_all(copies_g, ("dp", "expert"), split_axis=0, concat_axis=0, tiled=True),
    )
    return (routed_x, routed_g)


def collect(term_fn, total_rows, local_experts, capacity, features):
    dp_count = lax.axis_size("dp")
    ex_count = lax.axis_size("expert")
    experts = local_experts * ex_count
    whole_term = term_fn(0, total_rows).astype(jnp.bfloat16)
    arrived = lax.all_to_all(whole_term, ("dp", "expert"), split_axis=0, concat_axis=0, tiled=True)
    arrived = arrived.reshape(dp_count, experts, capacity, features)
    return jnp.sum(arrived.astype(jnp.float32), 0).astype(jnp.bfloat16)


def local(tokens, expert_ids, gate_weights, in_weights, out_weights, cotangent):
    ex_count = lax.axis_size("expert")
    local_experts = in_weights.shape[0]
    experts = local_experts * ex_count
    token_count = tokens.shape[0]
    features = tokens.shape[1]
    capacity = 2 * token_count // experts
    onehot = (expert_ids[:, None] == jnp.arange(experts, dtype=jnp.int32)[None, :]).astype(
        jnp.int32
    )
    rank_before = jnp.cumsum(onehot, 0) - onehot
    slot_index = jnp.sum(rank_before * onehot, 1)
    target = expert_ids * capacity + slot_index
    placer = (jnp.arange(experts * capacity, dtype=jnp.int32)[:, None] == target[None, :]).astype(
        jnp.bfloat16
    )
    out_grad = (gate_weights[:, None] * cotangent.astype(jnp.float32)).astype(jnp.bfloat16)
    sent_x = (
        jnp.dot(placer, tokens, preferred_element_type=jnp.float32)
        .astype(jnp.bfloat16)
        .reshape(experts, capacity, features)
    )
    sent_g = (
        jnp.dot(placer, out_grad, preferred_element_type=jnp.float32)
        .astype(jnp.bfloat16)
        .reshape(experts, capacity, features)
    )
    routed_x, routed_g = dispatch(sent_x, sent_g, local_experts)
    total_rows = routed_x.shape[0]
    pre_act = jnp.einsum("sfcd,fdh->sfch", routed_x, in_weights, preferred_element_type=jnp.float32)
    hidden = gelu_value(pre_act).astype(jnp.bfloat16)

    def forward_term(first_row, row_count):
        partial_value = jnp.einsum(
            "sfch,fhd->sfcd", hidden, out_weights, preferred_element_type=jnp.float32
        ).astype(jnp.bfloat16)
        return lax.optimization_barrier(partial_value).astype(jnp.float32)

    expert_out = collect(forward_term, total_rows, local_experts, capacity, features)
    token_out = jnp.einsum(
        "st,sd->td",
        placer,
        expert_out.reshape(experts * capacity, features),
        preferred_element_type=jnp.float32,
    )
    mixed = (gate_weights[:, None] * token_out).astype(jnp.bfloat16)
    gate_grad = jnp.sum(cotangent.astype(jnp.float32) * token_out, 1)
    hidden_back = jnp.einsum(
        "sfcd,fhd->sfch", routed_g, out_weights, preferred_element_type=jnp.float32
    )
    hidden_grad = (hidden_back * gelu_slope(pre_act)).astype(jnp.bfloat16)
    out_weights_grad = jnp.einsum(
        "sfch,sfcd->fhd", hidden, routed_g, preferred_element_type=jnp.float32
    ).astype(jnp.bfloat16)
    in_weights_grad = jnp.einsum(
        "sfcd,sfch->fdh", routed_x, hidden_grad, preferred_element_type=jnp.float32
    ).astype(jnp.bfloat16)

    def backward_term(first_row, row_count):
        partial_value = jnp.einsum(
            "sfch,fdh->sfcd", hidden_grad, in_weights, preferred_element_type=jnp.float32
        ).astype(jnp.bfloat16)
        return lax.optimization_barrier(partial_value).astype(jnp.float32)

    token_back = collect(backward_term, total_rows, local_experts, capacity, features)
    token_grad = jnp.einsum(
        "st,sd->td",
        placer,
        token_back.reshape(experts * capacity, features),
        preferred_element_type=jnp.float32,
    ).astype(jnp.bfloat16)
    return (mixed, gate_grad, token_grad, in_weights_grad, out_weights_grad)


def solution(mesh):
    in_specs = (
        P(("dp", "expert"), None),
        P(("dp", "expert")),
        P(("dp", "expert")),
        P("expert", None, "dp"),
        P("expert", "dp", None),
        P(("dp", "expert"), None),
    )
    out_specs = (
        P(("dp", "expert"), None),
        P(("dp", "expert")),
        P(("dp", "expert"), None),
        P("expert", None, "dp"),
        P("expert", "dp", None),
    )
    return jax.shard_map(local, mesh=mesh, in_specs=in_specs, out_specs=out_specs, check_vma=False)
```

profile of v0, /device:TPU:60, one launch (start us, length us, event | category | flops | bytes accessed | tf_op | source)
XLA Modules:
  0.0 494.4 jit_solution(1379574081296795589)
XLA Ops:
  0.6 0.0 copy-start
  0.6 0.8 fusion.40
  1.4 0.2 reduce_window_sum.11
  1.6 0.8 select_reduce_fusion
  2.5 0.7 multiply_add_fusion
  3.1 0.0 copy-done
  3.1 0.0 copy-start.4
  3.1 0.4 fusion.22
  3.6 4.3 broadcast_in_dim.9
  7.8 0.0 copy-start.2
  7.8 0.0 copy-start.6
  7.8 10.5 %all-to-all-start = ((bf16[128,2,8,2048]{3,2,1,0:T(8,128)(2,1)}), bf16[128,2,8,2048]{3,2,1,0:T(8,128)(2,1)}, u32[]{:S(2)}, u32[]{:S(2)}) async-start(bf16[128,2,8,2048]{3,2,1,0:T(8,128)(2,1)} %bitcast.69), calls=%async_computation | async-start | bytes 16777216 | tf_op jit(solution)/shard_map/all_to_all | solution.py:33
  18.4 0.0 copy-done.4
  18.4 0.0 copy-done.2
  18.4 0.0 copy-done.6
  18.4 0.5 fusion.23
  18.9 110.0 %all-to-all-done = bf16[128,2,8,2048]{3,2,1,0:T(8,128)(2,1)} async-done(((bf16[128,2,8,2048]{3,2,1,0:T(8,128)(2,1)}), bf16[128,2,8,2048]{3,2,1,0:T(8,128)(2,1)}, u32[]{:S(2)}, u32[]{:S(2)}) %all-to-all-start) | async-done | bytes 8388640 | tf_op jit(solution)/shard_map/all_to_all | solution.py:33
  128.9 4.3 broadcast_in_dim.11
  133.2 8.6 %all-to-all-start.2 = ((bf16[128,2,8,2048]{3,2,1,0:T(8,128)(2,1)}), bf16[128,2,8,2048]{3,2,1,0:T(8,128)(2,1)}, u32[]{:S(2)}, u32[]{:S(2)}) async-start(bf16[128,2,8,2048]{3,2,1,0:T(8,128)(2,1)} %bitcast.68), calls=%async_computation.2 | async-start | bytes 16777216 | tf_op jit(solution)/shard_map/all_to_all | solution.py:34
  141.8 0.0 copy-start.8
  141.8 11.5 %fusion = f32[2,128,8,512]{3,1,2,0:T(8,128)S(1)} fusion(bf16[128,2,8,2048]{3,2,1,0:T(8,128)(2,1)} %all-to-all-done, bf16[2,2048,512]{2,1,0:T(8,128)(2,1)} %param.9), kind=kOutput, calls=%fused_computation.4 | convolution fusion | flops 4294967296 | bytes 16777216 | tf_op jit(solution)/shard_map/sfcd,fdh->sfch/dot_general | solution.py:78
  153.3 0.0 copy-start.10
  153.3 2.0 copy-done.10
  155.3 0.0 copy-done.8
  155.3 6.7 %convert_bitcast_fusion.1 = bf16[128,2,8,2048]{3,0,2,1:T(8,128)(2,1)} fusion(bf16[2,512,2048]{2,1,0:T(8,128)(2,1)S(1)} %copy-done.8, f32[2,128,8,512]{3,1,2,0:T(8,128)S(1)} %fusion), kind=kOutput, calls=%fused_computation.7 | convolution fusion | flops 4304404480 | bytes 16777216 | tf_op jit(solution)/shard_map/sfch,fhd->sfcd/dot_general | solution.py:82
  162.0 11.2 %copy.20 = bf16[128,2,8,2048]{3,2,1,0:T(8,128)(2,1)} copy(bf16[128,2,8,2048]{3,0,2,1:T(8,128)(2,1)} %convert_bitcast_fusion.1) | data formatting | bytes 16777216 | tf_op jit(solution)/shard_map/optimization_barrier | solution.py:85
  173.2 77.8 %all-to-all-done.2 = bf16[128,2,8,2048]{3,2,1,0:T(8,128)(2,1)} async-done(((bf16[128,2,8,2048]{3,2,1,0:T(8,128)(2,1)}), bf16[128,2,8,2048]{3,2,1,0:T(8,128)(2,1)}, u32[]{:S(2)}, u32[]{:S(2)}) %all-to-all-start.2) | async-done | bytes 8388640 | tf_op jit(solution)/shard_map/all_to_all | solution.py:34
  251.1 8.8 %all-to-all-start.1 = ((bf16[128,2,8,2048]{3,2,1,0:T(8,128)(2,1)}), bf16[128,2,8,2048]{3,2,1,0:T(8,128)(2,1)}, u32[]{:S(2)}, u32[]{:S(2)}) async-start(bf16[128,2,8,2048]{3,2,1,0:T(8,128)(2,1)} %copy.20), calls=%async_computation.1 | async-start | bytes 16777216 | tf_op jit(solution)/shard_map/all_to_all | solution.py:44
  259.9 0.0 copy-start.9
  259.9 13.5 %fusion.11 = bf16[128,2,8,512]{3,0,2,1:T(8,128)(2,1)S(1)} fusion(f32[2,128,8,512]{3,1,2,0:T(8,128)} %copy-done.10, bf16[2,512,2048]{2,1,0:T(8,128)(2,1)} %param.10, bf16[128,2,8,2048]{3,2,1,0:T(8,128)(2,1)} %all-to-all-done.2), kind=kOutput, calls=%fused_computation.18 | convolution fusion | flops 4305453056 | bytes 18874368 | tf_op jit(solution)/shard_map/sfcd,fhd->sfch/dot_general | solution.py:96
  273.4 0.0 copy-done.9
  273.4 6.7 %convert_bitcast_fusion = bf16[128,2,8,2048]{3,0,2,1:T(8,128)(2,1)} fusion(bf16[128,2,8,512]{3,0,2,1:T(8,128)(2,1)S(1)} %fusion.11, bf16[2,2048,512]{2,1,0:T(8,128)(2,1)S(1)} %copy-done.9), kind=kOutput, calls=%fused_computation.6 | convolution fusion | flops 4299161600 | bytes 14680064 | tf_op jit(solution)/shard_map/sfch,fdh->sfcd/dot_general | solution.py:108
  280.1 11.2 %copy.22 = bf16[128,2,8,2048]{3,2,1,0:T(8,128)(2,1)} copy(bf16[128,2,8,2048]{3,0,2,1:T(8,128)(2,1)} %convert_bitcast_fusion) | data formatting | bytes 16777216 | tf_op jit(solution)/shard_map/optimization_barrier | solution.py:111
  291.3 18.6 %bitcast_convert_fusion = bf16[2,512,2048]{2,1,0:T(8,128)(2,1)} fusion(bf16[128,2,8,2048]{3,2,1,0:T(8,128)(2,1)} %all-to-all-done.2, f32[2,128,8,512]{3,1,2,0:T(8,128)} %copy-done.10), kind=kOutput, calls=%fused_computation | convolution fusion | flops 4302307328 | bytes 16777216 | tf_op jit(solution)/shard_map/sfch,sfcd->fhd/dot_general | solution.py:100
  309.9 59.3 %all-to-all-done.1 = bf16[128,2,8,2048]{3,2,1,0:T(8,128)(2,1)} async-done(((bf16[128,2,8,2048]{3,2,1,0:T(8,128)(2,1)}), bf16[128,2,8,2048]{3,2,1,0:T(8,128)(2,1)}, u32[]{:S(2)}, u32[]{:S(2)}) %all-to-all-start.1) | async-done | bytes 8388640 | tf_op jit(solution)/shard_map/all_to_all | solution.py:44
  369.2 8.2 %all-to-all-start.3 = ((bf16[128,2,8,2048]{3,2,1,0:T(8,128)(2,1)}), bf16[128,2,8,2048]{3,2,1,0:T(8,128)(2,1)}, u32[]{:S(2)}, u32[]{:S(2)}) async-start(bf16[128,2,8,2048]{3,2,1,0:T(8,128)(2,1)} %copy.22), calls=%async_computation.3 | async-start | bytes 16777216 | tf_op jit(solution)/shard_map/all_to_all | solution.py:44
  377.4 11.8 %bitcast_convert_fusion.1 = bf16[2,2048,512]{2,1,0:T(8,128)(2,1)} fusion(bf16[128,2,8,2048]{3,2,1,0:T(8,128)(2,1)} %all-to-all-done, bf16[128,2,8,512]{3,0,2,1:T(8,128)(2,1)S(1)} %fusion.11), kind=kOutput, calls=%fused_computation.1 | convolution fusion | flops 4297064448 | bytes 14680064 | tf_op jit(solution)/shard_map/sfcd,sfch->fdh/dot_general | solution.py:103
  389.2 0.0 copy-start.3
  389.2 0.0 copy-start.5
  389.2 0.0 copy-start.7
  389.2 5.2 %bitcast_reduce_fusion.1 = bf16[32,8,2048]{2,1,0:T(8,128)(2,1)S(1)} fusion(bf16[8,32,8,2048]{3,2,1,0:T(8,128)(2,1)} %bitcast.67), kind=kLoop, calls=%fused_computation.3 | loop fusion | flops 3670016 | bytes 9437184 | tf_op jit(solution)/shard_map/reduce_sum | solution.py:46
  394.4 0.0 copy-done.3
  394.4 0.0 copy-done.5
  394.4 0.0 copy-done.7
  394.4 1.8 fusion.29
  396.2 91.8 %all-to-all-done.3 = bf16[128,2,8,2048]{3,2,1,0:T(8,128)(2,1)} async-done(((bf16[128,2,8,2048]{3,2,1,0:T(8,128)(2,1)}), bf16[128,2,8,2048]{3,2,1,0:T(8,128)(2,1)}, u32[]{:S(2)}, u32[]{:S(2)}) %all-to-all-start.3) | async-done | bytes 8388640 | tf_op jit(solution)/shard_map/all_to_all | solution.py:44
  487.9 0.0 copy-start.1
  487.9 5.2 %bitcast_reduce_fusion = bf16[32,8,2048]{2,1,0:T(8,128)(2,1)S(1)} fusion(bf16[8,32,8,2048]{3,2,1,0:T(8,128)(2,1)} %bitcast.66), kind=kLoop, calls=%fused_computation.2 | loop fusion | flops 3670016 | bytes 9437184 | tf_op jit(solution)/shard_map/reduce_sum | solution.py:46
  493.1 1.1 convolution_convert_fusion.2
  494.2 0.0 copy-done.1
Async XLA Ops:
  0.6 2.5 copy-start
  3.1 15.2 %copy-start.4 = (s32[128]{0:T(128)}, s32[128]{0:T(128)S(1)}, u32[]{:S(2)}) copy-start(s32[128]{0:T(128)S(1)} %multiply_add_fusion) | copy-start | bytes 1540
  7.8 10.5 %copy-start.2 = (bf16[128,2048]{1,0:T(8,128)(2,1)S(1)}, bf16[128,2048]{1,0:T(8,128)(2,1)}, u32[]{:S(2)}) copy-start(bf16[128,2048]{1,0:T(8,128)(2,1)} %param.11) | copy-start | bytes 1572868
  7.8 10.6 %copy-start.6 = (f32[128]{0:T(128)S(1)}, f32[128]{0:T(128)}, u32[]{:S(2)}) copy-start(f32[128]{0:T(128)} %param.8) | copy-start | bytes 1540
  7.8 121.1 %all-to-all-start = ((bf16[128,2,8,2048]{3,2,1,0:T(8,128)(2,1)}), bf16[128,2,8,2048]{3,2,1,0:T(8,128)(2,1)}, u32[]{:S(2)}, u32[]{:S(2)}) async-start(bf16[128,2,8,2048]{3,2,1,0:T(8,128)(2,1)} %bitcast.69), calls=%async_computation | async-start | bytes 16777216 | tf_op jit(solution)/shard_map/all_to_all | solution.py:33
  133.2 117.9 %all-to-all-start.2 = ((bf16[128,2,8,2048]{3,2,1,0:T(8,128)(2,1)}), bf16[128,2,8,2048]{3,2,1,0:T(8,128)(2,1)}, u32[]{:S(2)}, u32[]{:S(2)}) async-start(bf16[128,2,8,2048]{3,2,1,0:T(8,128)(2,1)} %bitcast.68), calls=%async_computation.2 | async-start | bytes 16777216 | tf_op jit(solution)/shard_map/all_to_all | solution.py:34
  141.8 13.5 %copy-start.8 = (bf16[2,512,2048]{2,1,0:T(8,128)(2,1)S(1)}, bf16[2,512,2048]{2,1,0:T(8,128)(2,1)}, u32[]{:S(2)}) copy-start(bf16[2,512,2048]{2,1,0:T(8,128)(2,1)} %param.10) | copy-start | bytes 12582916
  153.3 2.0 copy-start.10
  251.1 118.1 %all-to-all-start.1 = ((bf16[128,2,8,2048]{3,2,1,0:T(8,128)(2,1)}), bf16[128,2,8,2048]{3,2,1,0:T(8,128)(2,1)}, u32[]{:S(2)}, u32[]{:S(2)}) async-start(bf16[128,2,8,2048]{3,2,1,0:T(8,128)(2,1)} %copy.20), calls=%async_computation.1 | async-start | bytes 16777216 | tf_op jit(solution)/shard_map/all_to_all | solution.py:44
  259.9 13.5 %copy-start.9 = (bf16[2,2048,512]{2,1,0:T(8,128)(2,1)S(1)}, bf16[2,2048,512]{2,1,0:T(8,128)(2,1)}, u32[]{:S(2)}) copy-start(bf16[2,2048,512]{2,1,0:T(8,128)(2,1)} %param.9) | copy-start | bytes 12582916
  369.2 118.8 %all-to-all-start.3 = ((bf16[128,2,8,2048]{3,2,1,0:T(8,128)(2,1)}), bf16[128,2,8,2048]{3,2,1,0:T(8,128)(2,1)}, u32[]{:S(2)}, u32[]{:S(2)}) async-start(bf16[128,2,8,2048]{3,2,1,0:T(8,128)(2,1)} %copy.22), calls=%async_computation.3 | async-start | bytes 16777216 | tf_op jit(solution)/shard_map/all_to_all | solution.py:44
  389.2 5.2 %copy-start.3 = (bf16[128,2048]{1,0:T(8,128)(2,1)S(1)}, bf16[128,2048]{1,0:T(8,128)(2,1)}, u32[]{:S(2)}) copy-start(bf16[128,2048]{1,0:T(8,128)(2,1)} %param.11) | copy-start | bytes 1572868
  389.2 5.2 %copy-start.5 = (s32[128]{0:T(128)S(1)}, s32[128]{0:T(128)}, u32[]{:S(2)}) copy-start(s32[128]{0:T(128)} %copy-done.4) | copy-start | bytes 1540
  389.2 5.2 %copy-start.7 = (f32[128]{0:T(128)S(1)}, f32[128]{0:T(128)}, u32[]{:S(2)}) copy-start(f32[128]{0:T(128)} %param.8) | copy-start | bytes 1540
  487.9 6.3 %copy-start.1 = (bf16[128,2048]{1,0:T(8,128)(2,1)S(1)}, bf16[128,2048]{1,0:T(8,128)(2,1)}, u32[]{:S(2)}) copy-start(bf16[128,2048]{1,0:T(8,128)(2,1)} %param.6) | copy-start | bytes 1572868
where the time goes:
time: 504 us; the launch traced here: 494 us
  waiting for transfers between devices  339 us (67%)
  matrix products  72.6 us (14%)
  starting transfers between devices  36.1 us (7%)
  local copies, waits for them, and re-layouts  33.1 us (7%)
  other arithmetic  12.8 us (3%)
    all_to_all x2, waiting for transfers between devices, collect(): lax.all_to_all(whole_term, ('dp', 'expert'), split_axis=0, concat_axis=0,...  151 us
    all_to_all x1, waiting for transfers between devices, dispatch(): lax.all_to_all(copies_x, ('dp', 'expert'), split_axis=0, concat_axis=0, t...  110 us
    all_to_all x1, waiting for transfers between devices, dispatch(): lax.all_to_all(copies_g, ('dp', 'expert'), split_axis=0, concat_axis=0, t...  77.8 us
    dot_general x1, matrix products, local(): jnp.einsum('sfch,sfcd->fhd', hidden, routed_g, preferred_element_type=jnp...  18.6 us
    all_to_all x2, starting transfers between devices, collect(): lax.all_to_all(whole_term, ('dp', 'expert'), split_axis=0, concat_axis=0,...  17 us
    dot_general x1, matrix products, local(): jnp.einsum('sfcd,fhd->sfch', routed_g, out_weights, preferred_element_typ...  13.5 us
    dot_general x1, matrix products, local(): jnp.einsum('sfcd,sfch->fdh', routed_x, hidden_grad, preferred_element_typ...  11.8 us
    dot_general x1, matrix products, local(): jnp.einsum('sfcd,fdh->sfch', routed_x, in_weights, preferred_element_type...  11.5 us
  transfers between devices with their start and end apart: 4, of which 4 were waited for; matrix products, arithmetic and copies ran while one was open for 20% of the time, Pallas kernels for 0%

commit v1 on v0

v1 whole, which is shorter than its diff:
```python
import jax
import jax.numpy as jnp
from jax import lax
from jax.sharding import PartitionSpec as P

root_half = 0.7071067811865476
inv_root_tau = 0.3989422804014327


def gelu_value(values):
    return 0.5 * values * (1.0 + lax.erf(values * root_half))


def gelu_slope(values):
    return (
        0.5 * (1.0 + lax.erf(values * root_half))
        + values * jnp.exp(-0.5 * values * values) * inv_root_tau
    )


def route(rows, local_experts):
    ex_count = lax.axis_size("expert")
    experts, capacity, features = rows.shape
    by_expert = rows.reshape(ex_count, local_experts, capacity, features)
    gathered = []
    for f in range(local_experts):
        swapped = lax.all_to_all(by_expert[:, f], "expert", split_axis=0, concat_axis=0, tiled=True)
        gathered.append(
            lax.all_gather(swapped.reshape(ex_count * capacity, features), "dp", axis=0, tiled=True)
        )
    return gathered


def route_back(term, capacity):
    ex_count = lax.axis_size("expert")
    summed = lax.psum_scatter(term.astype(jnp.bfloat16), "dp", scatter_dimension=0, tiled=True)
    return lax.all_to_all(
        summed.reshape(ex_count, capacity, term.shape[1]), "expert", split_axis=0, concat_axis=0, tiled=True
    )


def local(tokens, expert_ids, gate_weights, in_weights, out_weights, cotangent):
    ex_count = lax.axis_size("expert")
    local_experts = in_weights.shape[0]
    experts = local_experts * ex_count
    token_count = tokens.shape[0]
    features = tokens.shape[1]
    capacity = 2 * token_count // experts
    onehot = (expert_ids[:, None] == jnp.arange(experts, dtype=jnp.int32)[None, :]).astype(
        jnp.int32
    )
    rank_before = jnp.cumsum(onehot, 0) - onehot
    slot_index = jnp.sum(rank_before * onehot, 1)
    target = expert_ids * capacity + slot_index
    placer = (jnp.arange(experts * capacity, dtype=jnp.int32)[:, None] == target[None, :]).astype(
        jnp.bfloat16
    )
    out_grad = (gate_weights[:, None] * cotangent.astype(jnp.float32)).astype(jnp.bfloat16)

    def place(rows):
        return (
            jnp.dot(placer, rows, preferred_element_type=jnp.float32)
            .astype(jnp.bfloat16)
            .reshape(experts, capacity, features)
        )

    routed_x = route(place(tokens), local_experts)
    routed_g = route(place(out_grad), local_experts)
    dot = lambda a, b, dims: lax.dot_general(a, b, (dims, ((), ())), preferred_element_type=jnp.float32)
    fwd, bwd, in_grads, out_grads = [], [], [], []
    for f in range(local_experts):
        pre_act = dot(routed_x[f], in_weights[f], ((1,), (0,)))
        hidden = gelu_value(pre_act).astype(jnp.bfloat16)
        fwd.append(route_back(dot(hidden, out_weights[f], ((1,), (0,))), capacity))
        hidden_back = dot(routed_g[f], out_weights[f], ((1,), (1,)))
        hidden_grad = (hidden_back * gelu_slope(pre_act)).astype(jnp.bfloat16)
        bwd.append(route_back(dot(hidden_grad, in_weights[f], ((1,), (1,))), capacity))
        out_grads.append(dot(hidden, routed_g[f], ((0,), (0,))).astype(jnp.bfloat16))
        in_grads.append(dot(routed_x[f], hidden_grad, ((0,), (0,))).astype(jnp.bfloat16))

    def unplace(parts):
        rows = jnp.stack(parts, 1).reshape(experts * capacity, features)
        return jnp.einsum("st,sd->td", placer, rows, preferred_element_type=jnp.float32)

    token_out = unplace(fwd)
    mixed = (gate_weights[:, None] * token_out).astype(jnp.bfloat16)
    gate_grad = jnp.sum(cotangent.astype(jnp.float32) * token_out, 1)
    token_grad = unplace(bwd).astype(jnp.bfloat16)
    return (mixed, gate_grad, token_grad, jnp.stack(in_grads), jnp.stack(out_grads))


def solution(mesh):
    in_specs = (
        P(("dp", "expert"), None),
        P(("dp", "expert")),
        P(("dp", "expert")),
        P("expert", None, "dp"),
        P("expert", "dp", None),
        P(("dp", "expert"), None),
    )
    out_specs = (
        P(("dp", "expert"), None),
        P(("dp", "expert")),
        P(("dp", "expert"), None),
        P("expert", None, "dp"),
        P("expert", "dp", None),
    )
    return jax.shard_map(local, mesh=mesh, in_specs=in_specs, out_specs=out_specs, check_vma=False)
```

time: 504 us -> 346 us (0.69)
  the two profiles are of different devices: /device:TPU:60 before, /device:TPU:1 now
where the time goes in v1:
time: 346 us; the launch traced here: 341 us
  waiting for transfers between devices  163 us (47%)
  matrix products  66.6 us (19%)
  blocking collectives  56.7 us (16%)
  starting transfers between devices  27.2 us (8%)
  between operations  14.4 us (4%)
  other arithmetic  9.8 us (3%)
  local copies, waits for them, and re-layouts  3.89 us (1%)
    reduce_scatter x4, waiting for transfers between devices, route_back(): lax.psum_scatter(term.astype(jnp.bfloat16), 'dp', scatter_dimension=0, ti...  93.4 us
    dot_general x12, matrix products, local(): lax.dot_general(a, b, (dims, ((), ())), preferred_element_type=jnp.float32)  62.8 us
    all_gather x4, waiting for transfers between devices, route(): lax.all_gather(swapped.reshape(ex_count * capacity, features), 'dp', axis...  61.9 us
    all_to_all x4, blocking collectives, route(): lax.all_to_all(by_expert[:, f], 'expert', split_axis=0, concat_axis=0, ti...  56.7 us
    all_to_all x4, starting transfers between devices, route_back(): lax.all_to_all(summed.reshape(ex_count, capacity, term.shape[1]), 'expert...  26.7 us
    all_to_all x4, waiting for transfers between devices, route_back(): lax.all_to_all(summed.reshape(ex_count, capacity, term.shape[1]), 'expert...  7.3 us
  transfers between devices with their start and end apart: 12, of which 8 were waited for; matrix products, arithmetic and copies ran while one was open for 21% of the time, Pallas kernels for 0%

profile of v1, /device:TPU:1, one launch (start us, length us, event | category | flops | bytes accessed | tf_op | source)
XLA Modules:
  0.0 341.4 jit_solution(9415096691432978549)
XLA Ops:
  7.2 0.0 copy-start
  7.2 0.0 all-gather.5.cloned.1.call-start
  7.2 0.8 fusion.49
  8.0 0.2 reduce_window_sum.11
  8.2 0.8 select_reduce_fusion
  9.0 0.7 multiply_add_fusion
  9.7 0.4 convolution_convert_fusion.9
  10.1 0.1 slice_bitcast_fusion.3
  10.2 0.0 copy-start.5
  10.2 19.0 %all_to_all.40 = bf16[16,8,2048]{2,1,0:T(8,128)(2,1)} all-to-all(bf16[16,8,2048]{2,1,0:T(8,128)(2,1)S(1)} %get-tuple-element.9), channel_id=1, replica_groups=mesh['dp'=8,'expert'=16] {'expert'}, dimensions={0} | all-to-all | bytes 1048576 | tf_op jit(solution)/shard_map/all_to_all | solution.py:27
  29.2 0.0 all-gather.5.cloned.1.call-update
  29.2 0.0 all-gather.7.cloned.1.call-start
  29.3 13.0 %all_to_all.41 = bf16[16,8,2048]{2,1,0:T(8,128)(2,1)} all-to-all(bf16[16,8,2048]{2,1,0:T(8,128)(2,1)S(1)} %get-tuple-element.10), channel_id=1, replica_groups=mesh['dp'=8,'expert'=16] {'expert'}, dimensions={0} | all-to-all | bytes 1048576 | tf_op jit(solution)/shard_map/all_to_all | solution.py:27
  42.3 0.0 all-gather.7.cloned.1.call-update
  42.3 0.0 all-gather.9.cloned.1.call-start
  42.4 0.5 convolution_convert_fusion.8
  42.9 0.1 slice_bitcast_fusion.1
  43.0 12.3 %all_to_all.42 = bf16[16,8,2048]{2,1,0:T(8,128)(2,1)} all-to-all(bf16[16,8,2048]{2,1,0:T(8,128)(2,1)S(1)} %get-tuple-element.5), channel_id=1, replica_groups=mesh['dp'=8,'expert'=16] {'expert'}, dimensions={0} | all-to-all | bytes 1048576 | tf_op jit(solution)/shard_map/all_to_all | solution.py:27
  55.2 0.0 all-gather.9.cloned.1.call-update
  55.3 0.0 all-gather.11.cloned.1.call-start
  55.3 12.5 %all_to_all.43 = bf16[16,8,2048]{2,1,0:T(8,128)(2,1)} all-to-all(bf16[16,8,2048]{2,1,0:T(8,128)(2,1)S(1)} %get-tuple-element.6), channel_id=1, replica_groups=mesh['dp'=8,'expert'=16] {'expert'}, dimensions={0} | all-to-all | bytes 1048576 | tf_op jit(solution)/shard_map/all_to_all | solution.py:27
  67.8 0.0 all-gather.11.cloned.1.call-update
  67.8 0.0 reduce-scatter.5.cloned.1.call-start
  67.9 0.0 all-gather.5.cloned.1.call-done
  67.9 5.3 %fusion.26 = f32[1024,512]{1,0:T(8,128)S(1)} fusion(bf16[1024,2048]{1,0:T(8,128)(2,1)} %all-gather.5.cloned.1.call-done, bf16[2,2048,512]{2,1,0:T(8,128)(2,1)} %param.9), kind=kOutput, calls=%fused_computation.41 | convolution fusion | flops 2147483648 | bytes 8388608 | tf_op jit(solution)/shard_map/dot_general | solution.py:69
  73.3 1.4 copy-done.11
  74.6 3.9 %convolution_convert_fusion.3 = bf16[1024,2048]{1,0:T(8,128)(2,1)} fusion(bf16[2,512,2048]{2,1,0:T(8,128)(2,1)S(1)} %copy-done.6, f32[1024,512]{1,0:T(8,128)S(1)} %fusion.26), kind=kOutput, calls=%fused_computation.5 | convolution fusion | flops 2152202240 | bytes 8388608 | tf_op jit(solution)/shard_map/dot_general | solution.py:69
  78.5 0.0 reduce-scatter.5.cloned.1.call-update
  78.5 0.0 reduce-scatter.7.cloned.1.call-start
  78.6 16.1 %all-gather.7.cloned.1.call-done = bf16[1024,2048]{1,0:T(8,128)(2,1)} async-done(((bf16[128,2048]{1,0:T(8,128)(2,1)}), bf16[1024,2048]{1,0:T(8,128)(2,1)}) %all-gather.7.cloned.1.call-update) | async-done | bytes 4194320 | tf_op jit(solution)/shard_map/all_gather | solution.py:29
  94.7 5.3 %fusion.20 = f32[1024,512]{1,0:T(8,128)S(1)} fusion(bf16[1024,2048]{1,0:T(8,128)(2,1)} %all-gather.7.cloned.1.call-done, bf16[2,2048,512]{2,1,0:T(8,128)(2,1)} %param.9), kind=kOutput, calls=%fused_computation.35 | convolution fusion | flops 2147483648 | bytes 8388608 | tf_op jit(solution)/shard_map/dot_general | solution.py:69
  100.0 1.3 copy-done.13
  101.3 3.9 %convolution_convert_fusion.2 = bf16[1024,2048]{1,0:T(8,128)(2,1)} fusion(bf16[2,512,2048]{2,1,0:T(8,128)(2,1)S(1)} %copy-done.7, f32[1024,512]{1,0:T(8,128)S(1)} %fusion.20), kind=kOutput, calls=%fused_computation.4 | convolution fusion | flops 2152202240 | bytes 8388608 | tf_op jit(solution)/shard_map/dot_general | solution.py:69
  105.2 0.0 reduce-scatter.7.cloned.1.call-update
  105.3 0.2 reduce-scatter.9.cloned.1.call-start
  105.5 23.0 %all-gather.9.cloned.1.call-done = bf16[1024,2048]{1,0:T(8,128)(2,1)} async-done(((bf16[128,2048]{1,0:T(8,128)(2,1)}), bf16[1024,2048]{1,0:T(8,128)(2,1)}) %all-gather.9.cloned.1.call-update) | async-done | bytes 4194320 | tf_op jit(solution)/shard_map/all_gather | solution.py:29
  128.5 6.5 %fusion.9 = bf16[1024,512]{1,0:T(8,128)(2,1)S(1)} fusion(f32[1024,512]{1,0:T(8,128)} %copy-done.11, bf16[1024,2048]{1,0:T(8,128)(2,1)} %all-gather.9.cloned.1.call-done, bf16[2,512,2048]{2,1,0:T(8,128)(2,1)} %param.10), kind=kOutput, calls=%fused_computation.24 | convolution fusion | flops 2152726528 | bytes 9437184 | tf_op jit(solution)/shard_map/dot_general | solution.py:69
  135.0 4.4 %convolution_convert_fusion.1 = bf16[1024,2048]{1,0:T(8,128)(2,1)} fusion(bf16[1024,512]{1,0:T(8,128)(2,1)S(1)} %fusion.9, bf16[2,2048,512]{2,1,0:T(8,128)(2,1)S(1)} %copy-done.8), kind=kOutput, calls=%fused_computation.3 | convolution fusion | flops 2149580800 | bytes 7340032 | tf_op jit(solution)/shard_map/dot_general | solution.py:69
  139.4 0.0 reduce-scatter.9.cloned.1.call-update
  139.4 0.0 reduce-scatter.11.cloned.1.call-start
  139.4 22.8 %all-gather.11.cloned.1.call-done = bf16[1024,2048]{1,0:T(8,128)(2,1)} async-done(((bf16[128,2048]{1,0:T(8,128)(2,1)}), bf16[1024,2048]{1,0:T(8,128)(2,1)}) %all-gather.11.cloned.1.call-update) | async-done | bytes 4194320 | tf_op jit(solution)/shard_map/all_gather | solution.py:29
  162.2 6.5 %fusion.15 = bf16[1024,512]{1,0:T(8,128)(2,1)S(1)} fusion(f32[1024,512]{1,0:T(8,128)} %copy-done.13, bf16[1024,2048]{1,0:T(8,128)(2,1)} %all-gather.11.cloned.1.call-done, bf16[2,512,2048]{2,1,0:T(8,128)(2,1)} %param.10), kind=kOutput, calls=%fused_computation.30 | convolution fusion | flops 2152726528 | bytes 9437184 | tf_op jit(solution)/shard_map/dot_general | solution.py:69
  168.7 1.0 copy-done.14
  169.7 4.3 %convolution_convert_fusion = bf16[1024,2048]{1,0:T(8,128)(2,1)} fusion(bf16[1024,512]{1,0:T(8,128)(2,1)S(1)} %fusion.15, bf16[2,2048,512]{2,1,0:T(8,128)(2,1)S(1)} %copy-done.9), kind=kOutput, calls=%fused_computation.2 | convolution fusion | flops 2149580800 | bytes 7340032 | tf_op jit(solution)/shard_map/dot_general | solution.py:69
  174.0 0.0 reduce-scatter.11.cloned.1.call-update
  174.0 6.7 %fusion.3 = bf16[1,512,2048]{2,1,0:T(8,128)(2,1)} fusion(bf16[1024,2048]{1,0:T(8,128)(2,1)} %all-gather.11.cloned.1.call-done, f32[1024,512]{1,0:T(8,128)} %copy-done.13), kind=kOutput, calls=%fused_computation.15 | convolution fusion | flops 2151153664 | bytes 8388608 | tf_op jit(solution)/shard_map/dot_general | solution.py:69
  180.8 3.9 %fusion.2 = bf16[1,512,2048]{2,1,0:T(8,128)(2,1)} fusion(bf16[1024,2048]{1,0:T(8,128)(2,1)S(1)} %copy-done.10, f32[1024,512]{1,0:T(8,128)S(1)} %copy-done.12), kind=kOutput, calls=%fused_computation.14 | convolution fusion | flops 2151153664 | bytes 8388608 | tf_op jit(solution)/shard_map/dot_general | solution.py:69
  184.7 14.9 %reduce-scatter.5.cloned.1.call-done = bf16[128,2048]{1,0:T(8,128)(2,1)} async-done(((bf16[1024,2048]{1,0:T(8,128)(2,1)}), bf16[128,2048]{1,0:T(8,128)(2,1)}) %reduce-scatter.5.cloned.1.call-update) | async-done | bytes 524304 | tf_op jit(solution)/shard_map/reduce_scatter | solution.py:36
  199.6 6.6 %all-to-all-start.1 = ((bf16[16,8,2048]{2,1,0:T(8,128)(2,1)}), bf16[16,8,2048]{2,1,0:T(8,128)(2,1)S(1)}, u32[]{:S(2)}, u32[]{:S(2)}) async-start(bf16[16,8,2048]{2,1,0:T(8,128)(2,1)} %bitcast.86), calls=%async_computation.2 | async-start | bytes 1048576 | tf_op jit(solution)/shard_map/all_to_all | solution.py:37
  206.1 6.2 %fusion.1 = bf16[1,2048,512]{2,1,0:T(8,128)(2,1)} fusion(bf16[1024,2048]{1,0:T(8,128)(2,1)} %all-gather.7.cloned.1.call-done, bf16[1024,512]{1,0:T(8,128)(2,1)} %copy-done.14), kind=kOutput, calls=%fused_computation.13 | convolution fusion | flops 2148532224 | bytes 7340032 | tf_op jit(solution)/shard_map/dot_general | solution.py:69
  212.3 26.7 %reduce-scatter.7.cloned.1.call-done = bf16[128,2048]{1,0:T(8,128)(2,1)} async-done(((bf16[1024,2048]{1,0:T(8,128)(2,1)}), bf16[128,2048]{1,0:T(8,128)(2,1)}) %reduce-scatter.7.cloned.1.call-update) | async-done | bytes 524304 | tf_op jit(solution)/shard_map/reduce_scatter | solution.py:36
  239.0 6.8 %all-to-all-start.3 = ((bf16[16,8,2048]{2,1,0:T(8,128)(2,1)}), bf16[16,8,2048]{2,1,0:T(8,128)(2,1)S(1)}, u32[]{:S(2)}, u32[]{:S(2)}) async-start(bf16[16,8,2048]{2,1,0:T(8,128)(2,1)} %bitcast.85), calls=%async_computation.5 | async-start | bytes 1048576 | tf_op jit(solution)/shard_map/all_to_all | solution.py:37
  245.8 5.9 %fusion = bf16[1,2048,512]{2,1,0:T(8,128)(2,1)} fusion(bf16[1024,2048]{1,0:T(8,128)(2,1)} %all-gather.5.cloned.1.call-done, bf16[1024,512]{1,0:T(8,128)(2,1)S(1)} %fusion.9), kind=kOutput, calls=%fused_computation.12 | convolution fusion | flops 2148532224 | bytes 7340032 | tf_op jit(solution)/shard_map/dot_general | solution.py:69
  251.7 26.6 %reduce-scatter.9.cloned.1.call-done = bf16[128,2048]{1,0:T(8,128)(2,1)} async-done(((bf16[1024,2048]{1,0:T(8,128)(2,1)}), bf16[128,2048]{1,0:T(8,128)(2,1)}) %reduce-scatter.9.cloned.1.call-update) | async-done | bytes 524304 | tf_op jit(solution)/shard_map/reduce_scatter | solution.py:36
  278.3 6.7 %all-to-all-start.5 = ((bf16[16,8,2048]{2,1,0:T(8,128)(2,1)}), bf16[16,8,2048]{2,1,0:T(8,128)(2,1)S(1)}, u32[]{:S(2)}, u32[]{:S(2)}) async-start(bf16[16,8,2048]{2,1,0:T(8,128)(2,1)} %bitcast.84), calls=%async_computation.8 | async-start | bytes 1048576 | tf_op jit(solution)/shard_map/all_to_all | solution.py:37
  285.0 4.8 %pad_maximum_fusion = bf16[2,2048,512]{2,1,0:T(8,128)(2,1)} fusion(bf16[1,2048,512]{2,1,0:T(8,128)(2,1)} %fusion.1, bf16[1,2048,512]{2,1,0:T(8,128)(2,1)} %fusion), kind=kLoop, calls=%fused_computation | loop fusion | flops 2097152 | bytes 8388608 | tf_op jit(solution)/shard_map/stack | solution.py:89
  289.8 2.4 pad_maximum_fusion.1
  292.2 25.3 %reduce-scatter.11.cloned.1.call-done = bf16[128,2048]{1,0:T(8,128)(2,1)} async-done(((bf16[1024,2048]{1,0:T(8,128)(2,1)}), bf16[128,2048]{1,0:T(8,128)(2,1)}) %reduce-scatter.11.cloned.1.call-update) | async-done | bytes 524304 | tf_op jit(solution)/shard_map/reduce_scatter | solution.py:36
  317.4 6.7 %all-to-all-start.7 = ((bf16[16,8,2048]{2,1,0:T(8,128)(2,1)}), bf16[16,8,2048]{2,1,0:T(8,128)(2,1)S(1)}, u32[]{:S(2)}, u32[]{:S(2)}) async-start(bf16[16,8,2048]{2,1,0:T(8,128)(2,1)} %bitcast.83), calls=%async_computation.11 | async-start | bytes 1048576 | tf_op jit(solution)/shard_map/all_to_all | solution.py:37
  324.1 0.1 pad_maximum_fusion.2
  324.2 1.8 fusion.40
  326.0 7.3 %all-to-all-done.7 = bf16[16,8,2048]{2,1,0:T(8,128)(2,1)S(1)} async-done(((bf16[16,8,2048]{2,1,0:T(8,128)(2,1)}), bf16[16,8,2048]{2,1,0:T(8,128)(2,1)S(1)}, u32[]{:S(2)}, u32[]{:S(2)}) %all-to-all-start.7) | async-done | bytes 524320 | tf_op jit(solution)/shard_map/all_to_all | solution.py:37
  333.3 0.1 pad_maximum_fusion.3
  333.4 1.1 convolution_convert_fusion.10
  (28 shorter events, 0.1 us)
Async XLA Ops:
  7.2 2.5 copy-start
  7.2 60.7 %all-gather.5.cloned.1.call-start = ((), (), s32[]{:S(2)}) async-start(), calls=%async_computation.12 | async-start | bytes 4718592 | tf_op jit(solution)/shard_map/all_gather | solution.py:29
  10.2 32.1 %copy-start.4 = (bf16[128,2048]{1,0:T(8,128)(2,1)S(1)}, bf16[128,2048]{1,0:T(8,128)(2,1)}, u32[]{:S(2)}) copy-start(bf16[128,2048]{1,0:T(8,128)(2,1)} %param.11) | copy-start | bytes 1572868
  10.2 32.1 %copy-start.5 = (f32[128]{0:T(128)S(1)}, f32[128]{0:T(128)}, u32[]{:S(2)}) copy-start(f32[128]{0:T(128)} %param.8) | copy-start | bytes 1540
  29.2 65.5 %all-gather.7.cloned.1.call-start = ((), (), s32[]{:S(2)}) async-start(), calls=%async_computation.14 | async-start | bytes 4718592 | tf_op jit(solution)/shard_map/all_gather | solution.py:29
  42.3 86.2 %all-gather.9.cloned.1.call-start = ((), (), s32[]{:S(2)}) async-start(), calls=%async_computation.16 | async-start | bytes 4718592 | tf_op jit(solution)/shard_map/all_gather | solution.py:29
  55.3 106.9 %all-gather.11.cloned.1.call-start = ((), (), s32[]{:S(2)}) async-start(), calls=%async_computation.18 | async-start | bytes 4718592 | tf_op jit(solution)/shard_map/all_gather | solution.py:29
  67.8 131.7 %reduce-scatter.5.cloned.1.call-start = ((), (), s32[]{:S(2)}) async-start(), calls=%async_computation.13 | async-start | bytes 4718592 | tf_op jit(solution)/shard_map/reduce_scatter | solution.py:36
  67.9 6.7 %copy-start.6 = (bf16[2,512,2048]{2,1,0:T(8,128)(2,1)S(1)}, bf16[2,512,2048]{2,1,0:T(8,128)(2,1)}, u32[]{:S(2)}) copy-start(bf16[2,512,2048]{2,1,0:T(8,128)(2,1)} %param.10) | copy-start | bytes 12582916
  73.2 1.4 copy-start.11
  78.5 160.5 %reduce-scatter.7.cloned.1.call-start = ((), (), s32[]{:S(2)}) async-start(), calls=%async_computation.15 | async-start | bytes 4718592 | tf_op jit(solution)/shard_map/reduce_scatter | solution.py:36
  94.7 6.6 %copy-start.7 = (bf16[2,512,2048]{2,1,0:T(8,128)(2,1)S(1)}, bf16[2,512,2048]{2,1,0:T(8,128)(2,1)}, u32[]{:S(2)}) copy-start(bf16[2,512,2048]{2,1,0:T(8,128)(2,1)} %param.10) | copy-start | bytes 12582916
  100.0 1.3 copy-start.13
  105.3 173.0 %reduce-scatter.9.cloned.1.call-start = ((), (), s32[]{:S(2)}) async-start(), calls=%async_computation.17 | async-start | bytes 4718592 | tf_op jit(solution)/shard_map/reduce_scatter | solution.py:36
  128.5 6.5 %copy-start.8 = (bf16[2,2048,512]{2,1,0:T(8,128)(2,1)S(1)}, bf16[2,2048,512]{2,1,0:T(8,128)(2,1)}, u32[]{:S(2)}) copy-start(bf16[2,2048,512]{2,1,0:T(8,128)(2,1)} %param.9) | copy-start | bytes 12582916
  139.4 178.0 %reduce-scatter.11.cloned.1.call-start = ((), (), s32[]{:S(2)}) async-start(), calls=%async_computation.19 | async-start | bytes 4718592 | tf_op jit(solution)/shard_map/reduce_scatter | solution.py:36
  162.2 7.5 %copy-start.9 = (bf16[2,2048,512]{2,1,0:T(8,128)(2,1)S(1)}, bf16[2,2048,512]{2,1,0:T(8,128)(2,1)}, u32[]{:S(2)}) copy-start(bf16[2,2048,512]{2,1,0:T(8,128)(2,1)} %param.9) | copy-start | bytes 12582916
  168.7 1.0 copy-start.14
  174.0 6.8 %copy-start.10 = (bf16[1024,2048]{1,0:T(8,128)(2,1)S(1)}, bf16[1024,2048]{1,0:T(8,128)(2,1)}, u32[]{:S(2)}) copy-start(bf16[1024,2048]{1,0:T(8,128)(2,1)} %all-gather.9.cloned.1.call-done) | copy-start | bytes 12582916
  174.0 6.8 %copy-start.12 = (f32[1024,512]{1,0:T(8,128)S(1)}, f32[1024,512]{1,0:T(8,128)}, u32[]{:S(2)}) copy-start(f32[1024,512]{1,0:T(8,128)} %copy-done.11) | copy-start | bytes 6291460
  199.6 39.4 %all-to-all-start.1 = ((bf16[16,8,2048]{2,1,0:T(8,128)(2,1)}), bf16[16,8,2048]{2,1,0:T(8,128)(2,1)S(1)}, u32[]{:S(2)}, u32[]{:S(2)}) async-start(bf16[16,8,2048]{2,1,0:T(8,128)(2,1)} %bitcast.86), calls=%async_computation.2 | async-start | bytes 1048576 | tf_op jit(solution)/shard_map/all_to_all | solution.py:37
  239.0 39.3 %all-to-all-start.3 = ((bf16[16,8,2048]{2,1,0:T(8,128)(2,1)}), bf16[16,8,2048]{2,1,0:T(8,128)(2,1)S(1)}, u32[]{:S(2)}, u32[]{:S(2)}) async-start(bf16[16,8,2048]{2,1,0:T(8,128)(2,1)} %bitcast.85), calls=%async_computation.5 | async-start | bytes 1048576 | tf_op jit(solution)/shard_map/all_to_all | solution.py:37
  278.3 39.1 %all-to-all-start.5 = ((bf16[16,8,2048]{2,1,0:T(8,128)(2,1)}), bf16[16,8,2048]{2,1,0:T(8,128)(2,1)S(1)}, u32[]{:S(2)}, u32[]{:S(2)}) async-start(bf16[16,8,2048]{2,1,0:T(8,128)(2,1)} %bitcast.84), calls=%async_computation.8 | async-start | bytes 1048576 | tf_op jit(solution)/shard_map/all_to_all | solution.py:37
  285.0 4.8 %copy-start.2 = (bf16[1,512,2048]{2,1,0:T(8,128)(2,1)S(1)}, bf16[1,512,2048]{2,1,0:T(8,128)(2,1)}, u32[]{:S(2)}) copy-start(bf16[1,512,2048]{2,1,0:T(8,128)(2,1)} %fusion.3) | copy-start | bytes 6291460
  285.0 4.8 %copy-start.3 = (bf16[1,512,2048]{2,1,0:T(8,128)(2,1)S(1)}, bf16[1,512,2048]{2,1,0:T(8,128)(2,1)}, u32[]{:S(2)}) copy-start(bf16[1,512,2048]{2,1,0:T(8,128)(2,1)} %fusion.2) | copy-start | bytes 6291460
  317.4 15.9 %all-to-all-start.7 = ((bf16[16,8,2048]{2,1,0:T(8,128)(2,1)}), bf16[16,8,2048]{2,1,0:T(8,128)(2,1)S(1)}, u32[]{:S(2)}, u32[]{:S(2)}) async-start(bf16[16,8,2048]{2,1,0:T(8,128)(2,1)} %bitcast.83), calls=%async_computation.11 | async-start | bytes 1048576 | tf_op jit(solution)/shard_map/all_to_all | solution.py:37
  324.2 10.3 %copy-start.1 = (bf16[128,2048]{1,0:T(8,128)(2,1)S(1)}, bf16[128,2048]{1,0:T(8,128)(2,1)}, u32[]{:S(2)}) copy-start(bf16[128,2048]{1,0:T(8,128)(2,1)} %param.6) | copy-start | bytes 1572868
Sparse Core Ops, SparseCore 0:
  29.4 31.4 all-gather.4
  62.6 32.0 all-gather.6
  96.4 32.0 all-gather.8
  130.1 32.0 all-gather.10
  165.0 34.4 reduce-scatter.4
  202.4 36.5 reduce-scatter.6
  241.4 36.8 reduce-scatter.8
  280.7 36.6 reduce-scatter.10

commit v2 on v1

v2 whole, which is shorter than its diff:
```python
import functools

import jax
import jax.numpy as jnp
from jax import lax
from jax.experimental import pallas as pl
from jax.experimental.pallas import tpu as pltpu
from jax.sharding import PartitionSpec as P

root_half = 0.7071067811865476
inv_root_tau = 0.3989422804014327
MESH = pl.DeviceIdType.MESH
CAP = 8
UNIT = 2 * CAP
NY = 4
BF16, F32 = jnp.bfloat16, jnp.float32


def layer_kernel(
    plane,
    tok, cot, gate, ids, win_h, wout_h,
    mixed, ggrad, tgrad, dwin_h, dwout_h,
    X, G, win, wout, S, H, Pf, sib, rs, stage, aback, gown, sibx, sibg, sibids,
    swap_s, swap_r, w_s, a2a_s, a2a_r, ag_s, ag_r, sb_s, sb_r, ps_s, ps_r, rs_s, rs_r,
    bk_s, bk_r, fn_s, fn_r, out_s, credit,
):
    tokens, features = tok.shape
    block = UNIT * plane
    rows_all = NY * block
    hidden_width = win.shape[2]
    half_cols = features // 2
    tile_rows = rows_all // 2
    quarter = features // 4

    dp = lax.axis_index("dp")
    e = lax.axis_index("expert")
    y = dp // 2
    c = dp % 2
    o = 1 - c
    y_up, y_dn, y_far = (y + 1) % NY, (y + 3) % NY, (y + 2) % NY
    up, dn, twin = y_up * 2 + c, y_dn * 2 + c, y * 2 + o

    def remote(src, dst, ssem, rsem, to_dp, to_e=None):
        return pltpu.make_async_remote_copy(
            src_ref=src, dst_ref=dst, send_sem=ssem, recv_sem=rsem,
            device_id=(to_dp, e if to_e is None else to_e), device_id_type=MESH,
        )

    def wait_in(ref, sem):
        remote(ref, ref, sem, sem, dp).wait_recv()

    def wait_out(ref, sem):
        remote(ref, ref, sem, sem, dp).wait_send()

    def cols(h):
        return pl.ds(h * half_cols, half_cols)

    def block_rows(yb):
        return pl.ds(pl.multiple_of(yb * block, block), block)

    def unit_rows(start):
        return pl.ds(pl.multiple_of(start, UNIT), UNIT)

    load_in = pltpu.make_async_copy(win_h, win, w_s.at[0])
    load_out = pltpu.make_async_copy(wout_h, wout, w_s.at[1])
    load_in.start()
    load_out.start()

    barrier = pltpu.get_barrier_semaphore()

    def greet(k, carry):
        pl.semaphore_signal(barrier, inc=1, device_id=(dp, (e + k) % plane), device_id_type=MESH)
        return carry

    lax.fori_loop(1, plane, greet, 0)
    for other in (up, dn, twin):
        pl.semaphore_signal(barrier, inc=1, device_id=(other, e), device_id_type=MESH)

    gown[...] = (gate[...] * cot[...].astype(F32)).astype(BF16)

    def placer_of(id_rows, core):
        id_row = id_rows[0:1, :]
        n_experts = 2 * plane
        onehot = lax.broadcasted_iota(jnp.int32, (n_experts, tokens), 0) == id_row
        onehot_f = onehot.astype(F32)
        before = (
            lax.broadcasted_iota(jnp.int32, (tokens, tokens), 0)
            < lax.broadcasted_iota(jnp.int32, (tokens, tokens), 1)
        ).astype(F32).astype(BF16)
        rank = jnp.dot(onehot_f.astype(BF16), before, preferred_element_type=F32)
        slot = jnp.sum(rank * onehot_f, 0, keepdims=True).astype(jnp.int32)
        target = (id_row >> 1) * UNIT + core * CAP + slot
        target = jnp.where((id_row & 1) == c, target, -1)
        return (lax.broadcasted_iota(jnp.int32, (block, tokens), 0) == target).astype(F32).astype(BF16)

    placer_own = placer_of(ids[...], c)
    pl.semaphore_wait(barrier, plane + 2)

    swap = [
        remote(ids, sibids, swap_s.at[0], swap_r.at[0], twin),
        remote(tok, sibx, swap_s.at[1], swap_r.at[1], twin),
        remote(gown, sibg, swap_s.at[2], swap_r.at[2], twin),
    ]
    for copy in swap:
        copy.start()
    swap[0].wait_recv()
    placer_sib = placer_of(sibids[...], o)

    bufs = (X, G)
    own_src = (tok, gown)
    sib_src = (sibx, sibg)

    def place_and_send(a, h):
        placed = jnp.dot(placer_own, own_src[a][:, cols(h)], preferred_element_type=F32)
        placed += jnp.dot(placer_sib, sib_src[a][:, cols(h)], preferred_element_type=F32)
        stage[a, :, cols(h)] = placed.astype(BF16)

        def landing(sender):
            return bufs[a].at[c, unit_rows(y * block + sender * UNIT), cols(h)]

        pltpu.make_async_copy(stage.at[a, unit_rows(e * UNIT), cols(h)], landing(e), a2a_r.at[a, h]).start()

        def send(k, carry):
            to = (e + k) % plane
            remote(
                stage.at[a, unit_rows(to * UNIT), cols(h)], landing(e),
                a2a_s.at[a, h], a2a_r.at[a, h], dp, to,
            ).start()
            return carry

        lax.fori_loop(1, plane, send, 0)

    swap[1].wait_recv()
    place_and_send(0, 0)
    place_and_send(0, 1)
    swap[2].wait_recv()
    place_and_send(1, 0)
    place_and_send(1, 1)

    twin_pieces = ((y, 0), (y, 1), (y_dn, 0), (y_up, 1), (y_dn, 1), (y_up, 0), (y_far, 0), (y_far, 1))
    ring_pieces = ((y_dn, 0), (y_dn, 1), (y_up, 0), (y_up, 1), (y_far, 0), (y_far, 1))
    ring_to_twin = (2, 4, 5, 3, 6, 7)

    def piece(a, f, where):
        return bufs[a].at[f, block_rows(where[0]), cols(where[1])]

    def to_twin(a, k):
        ref = piece(a, c, twin_pieces[k])
        remote(ref, ref, sb_s.at[a, k], sb_r.at[a, k], twin).start()

    def send_own(a, h):
        ref = piece(a, c, (y, h))
        wait_in(ref, a2a_r.at[a, h])
        remote(ref, ref, ag_s.at[a, h], ag_r.at[a, h], up).start()
        remote(ref, ref, ag_s.at[a, 2 + h], ag_r.at[a, 2 + h], dn).start()
        to_twin(a, h)

    def arrived(a, i):
        ref = piece(a, c, ring_pieces[i])
        wait_in(ref, ag_r.at[a, i])
        if i == 0:
            remote(ref, ref, ag_s.at[a, 4], ag_r.at[a, 4], up).start()
        if i == 3:
            remote(ref, ref, ag_s.at[a, 5], ag_r.at[a, 5], dn).start()
        to_twin(a, ring_to_twin[i])

    def wait_twin(a):
        for k in range(8):
            wait_in(piece(a, o, twin_pieces[k]), sb_r.at[a, k])

    def wait_gather_sends(a):
        for h in range(2):
            wait_out(piece(a, c, (y, h)), ag_s.at[a, h])
            wait_out(piece(a, c, (y, h)), ag_s.at[a, 2 + h])
            wait_out(piece(a, c, (y, h)), ag_s.at[a, 4 + h])
        for k in range(8):
            wait_out(piece(a, c, (y, 0)), sb_s.at[a, k])

    send_own(0, 0)
    send_own(0, 1)
    arrived(0, 0)
    arrived(0, 3)
    send_own(1, 0)
    send_own(1, 1)
    arrived(0, 1)
    arrived(0, 2)
    arrived(0, 4)
    arrived(0, 5)

    def tile(t):
        return pl.ds(pl.multiple_of(t * tile_rows, tile_rows), tile_rows)

    def forward(f):
        def step(t, carry):
            rows = tile(t)
            pre = jnp.dot(X[f, rows, :], win[f], preferred_element_type=F32)
            cdf = 0.5 * (1.0 + lax.erf(pre * root_half))
            hid = (pre * cdf).astype(BF16)
            H[f, rows, :] = hid
            S[f, rows, :] = (cdf + pre * jnp.exp(-0.5 * pre * pre) * inv_root_tau).astype(BF16)
            for n in range(4):
                at = pl.ds(n * quarter, quarter)
                Pf[f, rows, at] = jnp.dot(hid, wout[f, :, at], preferred_element_type=F32).astype(BF16)
            return carry

        lax.fori_loop(0, 2, step, 0)

    sums = (Pf, G)

    def partial_to_twin(d):
        for t in range(2):
            remote(sums[d].at[o, tile(t)], sib.at[tile(t)], ps_s.at[d, t], ps_r.at[d, t], twin).start()

    def wait_partial_sends(d):
        for t in range(2):
            wait_out(sib.at[tile(t)], ps_s.at[d, t])

    def total(d, where):
        return sums[d].at[c, block_rows(where[0]), cols(where[1])]

    def rs_send(d, i, where, to):
        remote(total(d, where), rs.at[d, i], rs_s.at[d, i], rs_r.at[d, i], to).start()

    def add_twin(d, yb):
        rows = block_rows(yb)
        for h in range(2):
            sums[d][c, rows, cols(h)] = (
                sums[d][c, rows, cols(h)].astype(F32) + sib[rows, cols(h)].astype(F32)
            ).astype(BF16)

    def add_ring(d, where, i):
        wait_in(rs.at[d, i], rs_r.at[d, i])
        rows, h = block_rows(where[0]), where[1]
        sums[d][c, rows, cols(h)] = (
            sums[d][c, rows, cols(h)].astype(F32) + rs[d, i].astype(F32)
        ).astype(BF16)

    def reduce_start(d):
        for t in range(2):
            wait_in(sib.at[tile(t)], ps_r.at[d, t])
        add_twin(d, y_far)
        rs_send(d, 0, (y_far, 0), up)
        rs_send(d, 3, (y_far, 1), dn)
        add_twin(d, y_up)
        rs_send(d, 1, (y_up, 1), up)
        add_twin(d, y_dn)
        rs_send(d, 4, (y_dn, 0), dn)
        add_twin(d, y)

    def reduce_middle(d):
        add_ring(d, (y_up, 0), 0)
        rs_send(d, 2, (y_up, 0), up)
        add_ring(d, (y_dn, 1), 3)
        rs_send(d, 5, (y_dn, 1), dn)

    def reduce_end(d, h):
        ins = ((4, 2), (1, 5))[h]
        rows = block_rows(y)
        for i in ins:
            wait_in(rs.at[d, i], rs_r.at[d, i])
        sums[d][c, rows, cols(h)] = (
            sums[d][c, rows, cols(h)].astype(F32) + rs[d, ins[0]].astype(F32) + rs[d, ins[1]].astype(F32)
        ).astype(BF16)

        def leaving(to):
            return sums[d].at[c, unit_rows(y * block + to * UNIT), cols(h)]

        landing = aback.at[d, unit_rows(e * UNIT), cols(h)]
        pltpu.make_async_copy(leaving(e), landing, bk_r.at[d, h]).start()

        def send(k, carry):
            to = (e + k) % plane
            remote(leaving(to), landing, bk_s.at[d, h], bk_r.at[d, h], dp, to).start()
            return carry

        lax.fori_loop(1, plane, send, 0)

    kept = (mixed, tgrad)
    other_sum = (sibx, sibg)

    def unplace(d, h):
        wait_in(aback.at[d, :, cols(h)], bk_r.at[d, h])
        routed = aback[d, :, cols(h)]
        dims = (((0,), (0,)), ((), ()))
        leave = stage.at[d, pl.ds(0, tokens), cols(h)]
        leave[...] = lax.dot_general(placer_sib, routed, dims, preferred_element_type=F32).astype(BF16)
        remote(leave, other_sum[d].at[:, cols(h)], fn_s.at[d, h], fn_r.at[d, h], twin).start()
        kept[d][:, cols(h)] = lax.dot_general(placer_own, routed, dims, preferred_element_type=F32).astype(BF16)

    def token_rows(d, h):
        wait_in(other_sum[d].at[:, cols(h)], fn_r.at[d, h])
        return kept[d][:, cols(h)].astype(F32) + other_sum[d][:, cols(h)].astype(F32)

    load_in.wait()
    load_out.wait()
    wait_twin(0)
    forward(o)
    partial_to_twin(0)
    arrived(1, 0)
    arrived(1, 3)
    forward(c)
    arrived(1, 1)
    arrived(1, 2)
    reduce_start(0)
    pl.semaphore_signal(credit, inc=1, device_id=(twin, e), device_id_type=MESH)
    arrived(1, 4)
    arrived(1, 5)

    transposed = (((1,), (1,)), ((), ()))
    over_rows = (((0,), (0,)), ((), ()))

    def hidden_back(f):
        def step(t, carry):
            rows = tile(t)
            back = lax.dot_general(G[f, rows, :], wout[f], transposed, preferred_element_type=F32)
            H[f, rows, :] = (back * S[f, rows, :].astype(F32)).astype(BF16)
            return carry

        lax.fori_loop(0, 2, step, 0)

    def token_back(f):
        def step(t, carry):
            rows = tile(t)
            for n in range(4):
                at = pl.ds(n * quarter, quarter)
                G[f, rows, at] = lax.dot_general(
                    H[f, rows, :], win[f, at, :], transposed, preferred_element_type=F32
                ).astype(BF16)
            return carry

        lax.fori_loop(0, 2, step, 0)

    def out_weights_tile(f, n):
        at = pl.ds(pl.multiple_of(n * quarter, quarter), quarter)
        Pf[o, pl.ds(pl.multiple_of(f * hidden_width, hidden_width), hidden_width), at] = lax.dot_general(
            H[f], G[f, :, at], over_rows, preferred_element_type=F32
        ).astype(BF16)

    def in_weights_spot(f, m):
        return (
            o,
            pl.ds(pl.multiple_of(f * quarter, quarter), quarter),
            pl.ds(pl.multiple_of(m * hidden_width, hidden_width), hidden_width),
        )

    def in_weights_tile(f, m):
        at = pl.ds(pl.multiple_of(m * quarter, quarter), quarter)
        Pf[in_weights_spot(f, m)] = lax.dot_general(
            X[f, :, at], H[f], over_rows, preferred_element_type=F32
        ).astype(BF16)

    wait_twin(1)
    wait_partial_sends(0)

    def out_tiles(f):
        def step(n, carry):
            out_weights_tile(f, n)
            return carry

        lax.fori_loop(0, 4, step, 0)

    out_tiles(o)
    reduce_middle(0)
    out_tiles(c)
    out_copies = [
        pltpu.make_async_copy(Pf.at[o, pl.ds(f * hidden_width, hidden_width)], dwout_h.at[f], out_s.at[f])
        for f in range(2)
    ]
    for copy in out_copies:
        copy.start()
    hidden_back(o)
    hidden_back(c)
    wait_gather_sends(1)
    token_back(o)
    pl.semaphore_wait(credit, 1)
    partial_to_twin(1)
    token_back(c)
    reduce_start(1)
    reduce_end(0, 0)
    reduce_end(0, 1)
    for copy in out_copies:
        copy.wait()

    def in_tiles(f):
        def step(m, carry):
            in_weights_tile(f, m)
            return carry

        lax.fori_loop(0, 4, step, 0)
        for m in range(4):
            pltpu.make_async_copy(
                Pf.at[in_weights_spot(f, m)], dwin_h.at[f, pl.ds(m * quarter, quarter)], out_s.at[2 + 4 * f + m]
            ).start()

    sent_rows = UNIT * (plane - 1)
    for a in range(2):
        for h in range(2):
            wait_out(stage.at[a, pl.ds(0, sent_rows), cols(h)], a2a_s.at[a, h])
    for copy in swap:
        copy.wait_send()
    wait_partial_sends(1)

    in_tiles(0)
    reduce_middle(1)
    unplace(0, 0)
    unplace(0, 1)
    in_tiles(1)
    gate_total = jnp.zeros((tokens, 1), F32)
    for h in range(2):
        out_rows = token_rows(0, h)
        gate_total += jnp.sum(cot[:, cols(h)].astype(F32) * out_rows, 1, keepdims=True)
        mixed[:, cols(h)] = (gate[...] * out_rows).astype(BF16)
    ggrad[...] = gate_total
    reduce_end(1, 0)
    reduce_end(1, 1)
    unplace(1, 0)
    unplace(1, 1)
    for h in range(2):
        tgrad[:, cols(h)] = token_rows(1, h).astype(BF16)

    wait_gather_sends(0)
    for f in range(2):
        for m in range(4):
            pltpu.make_async_copy(
                Pf.at[in_weights_spot(f, m)], dwin_h.at[f, pl.ds(m * quarter, quarter)], out_s.at[2 + 4 * f + m]
            ).wait()
    for d in range(2):
        for i in range(6):
            wait_out(rs.at[d, i], rs_s.at[d, i])
        for h in range(2):
            wait_out(aback.at[d, pl.ds(0, sent_rows), cols(h)], bk_s.at[d, h])
            wait_out(stage.at[d, pl.ds(0, tokens), cols(h)], fn_s.at[d, h])


def local(tokens, expert_ids, gate_weights, in_weights, out_weights, cotangent):
    plane = lax.axis_size("expert")
    count, features = tokens.shape
    hidden_width = in_weights.shape[2]
    block = UNIT * plane
    rows_all = NY * block
    half_cols = features // 2
    vmem = pl.BlockSpec(memory_space=pltpu.VMEM)
    hbm = pl.BlockSpec(memory_space=pl.ANY)
    dma = pltpu.SemaphoreType.DMA
    mixed, gate_grad, token_grad, in_grad, out_grad = pl.pallas_call(
        functools.partial(layer_kernel, plane),
        out_shape=(
            jax.ShapeDtypeStruct((count, features), BF16),
            jax.ShapeDtypeStruct((count, 1), F32),
            jax.ShapeDtypeStruct((count, features), BF16),
            jax.ShapeDtypeStruct(in_weights.shape, BF16),
            jax.ShapeDtypeStruct(out_weights.shape, BF16),
        ),
        in_specs=[vmem, vmem, vmem, vmem, hbm, hbm],
        out_specs=(vmem, vmem, vmem, hbm, hbm),
        scratch_shapes=[
            pltpu.VMEM((2, rows_all, features), BF16),
            pltpu.VMEM((2, rows_all, features), BF16),
            pltpu.VMEM(in_weights.shape, BF16),
            pltpu.VMEM(out_weights.shape, BF16),
            pltpu.VMEM((2, rows_all, hidden_width), BF16),
            pltpu.VMEM((2, rows_all, hidden_width), BF16),
                pltpu.VMEM((2, rows_all, features), BF16),
            pltpu.VMEM((rows_all, features), BF16),
            pltpu.VMEM((2, 6, block, half_cols), BF16),
            pltpu.VMEM((2, block, features), BF16),
            pltpu.VMEM((2, block, features), BF16),
            pltpu.VMEM((count, features), BF16),
            pltpu.VMEM((count, features), BF16),
            pltpu.VMEM((count, features), BF16),
            pltpu.VMEM((8, count), jnp.int32),
            dma((3,)), dma((3,)), dma((2,)),
            dma((2, 2)), dma((2, 2)),
            dma((2, 6)), dma((2, 6)),
            dma((2, 8)), dma((2, 8)),
            dma((2, 2)), dma((2, 2)),
            dma((2, 6)), dma((2, 6)),
            dma((2, 2)), dma((2, 2)),
            dma((2, 2)), dma((2, 2)),
            dma((10,)),
            pltpu.SemaphoreType.REGULAR,
        ],
        compiler_params=pltpu.CompilerParams(
            collective_id=0, has_side_effects=True, vmem_limit_bytes=60 * 1024 * 1024
        ),
    )(
        tokens, cotangent, gate_weights[:, None],
        jnp.broadcast_to(expert_ids[None], (8, count)), in_weights, out_weights,
    )
    return mixed, gate_grad[:, 0], token_grad, in_grad, out_grad


def solution(mesh):
    in_specs = (
        P(("dp", "expert"), None),
        P(("dp", "expert")),
        P(("dp", "expert")),
        P("expert", None, "dp"),
        P("expert", "dp", None),
        P(("dp", "expert"), None),
    )
    out_specs = (
        P(("dp", "expert"), None),
        P(("dp", "expert")),
        P(("dp", "expert"), None),
        P("expert", None, "dp"),
        P("expert", "dp", None),
    )
    return jax.shard_map(local, mesh=mesh, in_specs=in_specs, out_specs=out_specs, check_vma=False)
```

time: 346 us -> 192 us (0.55); the launches traced: 341 us -> 192 us
  Pallas kernels: 0 us -> 177 us
  waiting for transfers between devices: 163 us -> 0 us
  matrix products: 66.6 us -> 0 us
  blocking collectives: 56.7 us -> 0 us
  starting transfers between devices: 27.2 us -> 0 us
  between operations: 14.4 us -> 0.64 us
  local copies, waits for them, and re-layouts: 3.89 us -> 13 us
  other arithmetic: 9.8 us -> 1.47 us
    pallas_call x0 -> x1, Pallas kernels: none -> 177 us  [local(): pl.pallas_call(functools.partial(layer_kernel, plane), out_shape=(jax.Sha...]
    reduce_scatter x4 -> x0, waiting for transfers between devices: 93.4 us -> none  [route_back(): lax.psum_scatter(term.astype(jnp.bfloat16), 'dp', scatter_dimension=0, ti...]
    dot_general x16 -> x0, matrix products: 66.6 us -> none  [the longest x12 62.8 us: local(): lax.dot_general(a, b, (dims, ((), ())), preferred_element_type=jnp.float32)]
    all_gather x4 -> x0, waiting for transfers between devices: 61.9 us -> none  [route(): lax.all_gather(swapped.reshape(ex_count * capacity, features), 'dp', axis...]
    all_to_all x4 -> x0, blocking collectives: 56.7 us -> none  [route(): lax.all_to_all(by_expert[:, f], 'expert', split_axis=0, concat_axis=0, ti...]
    all_to_all x4 -> x0, starting transfers between devices: 26.7 us -> none  [route_back(): lax.all_to_all(summed.reshape(ex_count, capacity, term.shape[1]), 'expert...]
    another operation x5 -> x0, other arithmetic: 7.52 us -> none  [the longest x1 4.77 us: local(): jnp.stack(in_grads)]
    all_to_all x4 -> x0, waiting for transfers between devices: 7.3 us -> none  [route_back(): lax.all_to_all(summed.reshape(ex_count, capacity, term.shape[1]), 'expert...]
  transfers between devices with their start and end apart: 12 -> 0, of which waited for: 8 -> 0; matrix products, arithmetic and copies ran while one was open for 21% -> 0% of each run, Pallas kernels for 0% -> 0%
where the time goes in v2:
time: 192 us
  Pallas kernels  177 us (92%)
  local copies, waits for them, and re-layouts  13 us (7%)
    pallas_call x1, Pallas kernels, local(): pl.pallas_call(functools.partial(layer_kernel, plane), out_shape=(jax.Sha...  177 us
    unnamed x6, local copies, waits for them, and re-layouts  10.4 us

profile of v2, /device:TPU:1, one launch (start us, length us, event | category | flops | bytes accessed | tf_op | source)
XLA Modules:
  0.0 191.7 jit_solution(13252383883051692901)
XLA Ops:
  0.6 1.2 broadcast_in_dim.10.ids
  1.9 1.4 copy.12.gate
  3.3 176.5 %shard_map.101 = (bf16[128,2048]{1,0:T(8,128)(2,1)}, f32[128,1]{1,0:T(8,128)}, bf16[128,2048]{1,0:T(8,128)(2,1)}, bf16[2,2048,512]{2,1,0:T(8,128)(2,1)}, bf16[2,512,2048]{2,1,0:T(8,128)(2,1)}) custom-call(bf16[128,2048]{1,0:T(8,128)(2,1)} %tok.1, bf16[128,2048]{1,0:T(8,128)(2,1)} %cot.1, f32[128,1]{1,0:T(8,128)} %copy.12.gate, ...), custom_call_target="tpu_custom_call" | custom-call | tf_op jit(solution)/shard_map/pallas_call | solution.py:445
  179.8 1.5 reduce
  181.2 1.9 copy.17
  183.1 1.9 copy.18
  185.0 0.0 copy-start
  185.0 4.6 %copy.19 = bf16[2,2048,512]{2,1,0:T(8,128)(2,1)} copy(bf16[2,2048,512]{2,1,0:T(8,128)(2,1)} %get-tuple-element.23) | data formatting | bytes 8388608
  189.6 0.0 copy-done
  189.6 2.0 %copy.20 = bf16[2,512,2048]{2,1,0:T(8,128)(2,1)} copy(bf16[2,512,2048]{2,1,0:T(8,128)(2,1)S(1)} %copy-done) | data formatting | bytes 8388608
Async XLA Ops:
  185.0 4.6 %copy-start = (bf16[2,512,2048]{2,1,0:T(8,128)(2,1)S(1)}, bf16[2,512,2048]{2,1,0:T(8,128)(2,1)}, u32[]{:S(2)}) copy-start(bf16[2,512,2048]{2,1,0:T(8,128)(2,1)} %get-tuple-element.24) | copy-start | bytes 12582916

commit v3 on v1

v3 whole, which is shorter than its diff:
```python
import functools

import jax
import jax.numpy as jnp
from jax import lax
from jax.experimental import pallas as pl
from jax.experimental.pallas import tpu as pltpu
from jax.sharding import PartitionSpec as P

root_half = 0.7071067811865476
inv_root_tau = 0.3989422804014327
MESH = pl.DeviceIdType.MESH
CAP = 8
UNIT = 2 * CAP
NY = 4
CHUNKS = 4
BF16, F32 = jnp.bfloat16, jnp.float32


def layer_kernel(
    plane,
    tok, cot, gate, ids, win_h, wout_h,
    mixed, ggrad, tgrad, dwin_h, dwout_h,
    XG, win, wout, S, H, Pf, sib, rs, stage, aback, gown, sibx, sibg, sibids,
    swap_s, swap_r, w_s, a2a_s, a2a_r, ag_s, ag_r, sb_s, sb_r, ps_s, ps_r, rs_s, rs_r,
    bk_s, bk_r, fn_s, fn_r, out_s, credit,
):
    tokens, features = tok.shape
    block = UNIT * plane
    rows_all = NY * block
    hidden_width = win.shape[2]
    tile_rows = rows_all // 2
    quarter = features // CHUNKS
    eighth = quarter // 2
    X, G = XG.at[0], XG.at[1]

    dp = lax.axis_index("dp")
    e = lax.axis_index("expert")
    y = dp // 2
    c = dp % 2
    o = 1 - c
    y_up, y_dn, y_far = (y + 1) % NY, (y + 3) % NY, (y + 2) % NY
    up, dn, twin = y_up * 2 + c, y_dn * 2 + c, y * 2 + o

    def remote(src, dst, ssem, rsem, to_dp, to_e=None):
        return pltpu.make_async_remote_copy(
            src_ref=src, dst_ref=dst, send_sem=ssem, recv_sem=rsem,
            device_id=(to_dp, e if to_e is None else to_e), device_id_type=MESH,
        )

    def wait_in(ref, sem):
        remote(ref, ref, sem, sem, dp).wait_recv()

    def wait_out(ref, sem):
        remote(ref, ref, sem, sem, dp).wait_send()

    def cols(k):
        return pl.ds(k * quarter, quarter)

    def part(k, h):
        return pl.ds(k * quarter + h * eighth, eighth)

    def block_rows(yb):
        return pl.ds(pl.multiple_of(yb * block, block), block)

    def unit_rows(start):
        return pl.ds(pl.multiple_of(start, UNIT), UNIT)

    load_in = pltpu.make_async_copy(win_h, win, w_s.at[0])
    load_out = pltpu.make_async_copy(wout_h, wout, w_s.at[1])

    barrier = pltpu.get_barrier_semaphore()

    def greet(k, carry):
        pl.semaphore_signal(barrier, inc=1, device_id=(dp, (e + k) % plane), device_id_type=MESH)
        return carry

    for other in (twin, up, dn):
        pl.semaphore_signal(barrier, inc=1, device_id=(other, e), device_id_type=MESH)
    lax.fori_loop(1, plane, greet, 0)

    diagonal = lax.broadcasted_iota(jnp.int32, (tokens, tokens), 0) == lax.broadcasted_iota(
        jnp.int32, (tokens, tokens), 1
    )
    gate_col = jnp.sum(jnp.where(diagonal, gate[...], 0.0), 1, keepdims=True)
    gown[...] = (gate_col * cot[...].astype(F32)).astype(BF16)

    def placer_of(id_row, core):
        n_experts = 2 * plane
        onehot = lax.broadcasted_iota(jnp.int32, (n_experts, tokens), 0) == id_row
        onehot_f = onehot.astype(F32)
        before = (
            lax.broadcasted_iota(jnp.int32, (tokens, tokens), 0)
            < lax.broadcasted_iota(jnp.int32, (tokens, tokens), 1)
        ).astype(F32).astype(BF16)
        rank = jnp.dot(onehot_f.astype(BF16), before, preferred_element_type=F32)
        slot = jnp.sum(rank * onehot_f, 0, keepdims=True).astype(jnp.int32)
        target = (id_row >> 1) * UNIT + core * CAP + slot
        target = jnp.where((id_row & 1) == c, target, -1)
        return (lax.broadcasted_iota(jnp.int32, (block, tokens), 0) == target).astype(F32).astype(BF16)

    placer_own = placer_of(ids[...], c)
    pl.semaphore_wait(barrier, plane + 2)

    swap = [
        remote(ids, sibids, swap_s.at[0], swap_r.at[0], twin),
        remote(tok, sibx, swap_s.at[1], swap_r.at[1], twin),
        remote(gown, sibg, swap_s.at[2], swap_r.at[2], twin),
    ]
    for copy in swap:
        copy.start()
    load_in.start()
    load_out.start()
    swap[0].wait_recv()
    placer_sib = placer_of(sibids[...], o)

    own_src = (tok, gown)
    sib_src = (sibx, sibg)
    chunks = [(a, k) for a in range(2) for k in range(CHUNKS)]

    def place(q):
        a, k = chunks[q]
        placed = jnp.dot(placer_own, own_src[a][:, cols(k)], preferred_element_type=F32)
        placed += jnp.dot(placer_sib, sib_src[a][:, cols(k)], preferred_element_type=F32)
        stage[a, :, cols(k)] = placed.astype(BF16)

    def scatter(q):
        a, k = chunks[q]
        landing = XG.at[a, c, unit_rows(y * block + e * UNIT), cols(k)]
        pltpu.make_async_copy(stage.at[a, unit_rows(e * UNIT), cols(k)], landing, a2a_r.at[a, k]).start()

        def send(step, carry):
            to = (e + step) % plane
            remote(
                stage.at[a, unit_rows(to * UNIT), cols(k)], landing, a2a_s.at[a, k], a2a_r.at[a, k], dp, to
            ).start()
            return carry

        lax.fori_loop(1, plane, send, 0)

    ring_pieces = ((y_dn, 0), (y_dn, 1), (y_up, 0), (y_up, 1), (y_far, 0), (y_far, 1))

    def piece(q, f, where):
        a, k = chunks[q]
        return XG.at[a, f, block_rows(where[0]), part(k, where[1])]

    def to_twin(q, n, where):
        a, k = chunks[q]
        ref = piece(q, c, where)
        remote(ref, ref, sb_s.at[a, k, n], sb_r.at[a, k, n], twin).start()

    def send_own(q):
        a, k = chunks[q]
        wait_in(XG.at[a, c, block_rows(y), cols(k)], a2a_r.at[a, k])
        for h in range(2):
            for n, to in ((h, up), (2 + h, dn)):
                ref = piece(q, c, (y, h))
                remote(ref, ref, ag_s.at[a, k, n], ag_r.at[a, k, n], to).start()
        for h in range(2):
            to_twin(q, 6 + h, (y, h))

    def forward_on(q):
        a, k = chunks[q]
        for i, n, to in ((0, 4, up), (3, 5, dn)):
            ref = piece(q, c, ring_pieces[i])
            wait_in(ref, ag_r.at[a, k, i])
            remote(ref, ref, ag_s.at[a, k, n], ag_r.at[a, k, n], to).start()
            to_twin(q, i, ring_pieces[i])

    def take_rest(q):
        a, k = chunks[q]
        for i in (1, 2, 4, 5):
            wait_in(piece(q, c, ring_pieces[i]), ag_r.at[a, k, i])
            to_twin(q, i, ring_pieces[i])

    def wait_twin(a):
        for k in range(CHUNKS):
            q = a * CHUNKS + k
            for n, where in enumerate(ring_pieces + ((y, 0), (y, 1))):
                wait_in(piece(q, o, where), sb_r.at[a, k, n])

    def wait_gather_sends(a):
        for k in range(CHUNKS):
            q = a * CHUNKS + k
            for n in range(6):
                wait_out(piece(q, c, (y, 0)), ag_s.at[a, k, n])
            for n in range(8):
                wait_out(piece(q, c, (y, 0)), sb_s.at[a, k, n])

    def tile(t):
        return pl.ds(pl.multiple_of(t * tile_rows, tile_rows), tile_rows)

    def forward(f, t):
        rows = tile(t)
        pre = jnp.dot(X[f, rows, :], win[f], preferred_element_type=F32)
        cdf = 0.5 * (1.0 + lax.erf(pre * root_half))
        hid = (pre * cdf).astype(BF16)
        H[f, rows, :] = hid
        S[f, rows, :] = (cdf + pre * jnp.exp(-0.5 * pre * pre) * inv_root_tau).astype(BF16)
        for k in range(CHUNKS):
            Pf[f, rows, cols(k)] = jnp.dot(hid, wout[f, :, cols(k)], preferred_element_type=F32).astype(BF16)

    sums = (Pf, G)

    def partial_to_twin(d, k):
        remote(sums[d].at[o, :, cols(k)], sib.at[:, cols(k)], ps_s.at[d, k], ps_r.at[d, k], twin).start()

    def wait_partial_sends(d):
        for k in range(CHUNKS):
            wait_out(sib.at[:, cols(k)], ps_s.at[d, k])

    def rs_send(d, k, i, where, to):
        ref = sums[d].at[c, block_rows(where[0]), part(k, where[1])]
        remote(ref, rs.at[d, k, i], rs_s.at[d, k, i], rs_r.at[d, k, i], to).start()

    def add_twin(d, k, yb):
        rows = block_rows(yb)
        sums[d][c, rows, cols(k)] = (
            sums[d][c, rows, cols(k)].astype(F32) + sib[rows, cols(k)].astype(F32)
        ).astype(BF16)

    def add_ring(d, k, where, i):
        wait_in(rs.at[d, k, i], rs_r.at[d, k, i])
        rows, at = block_rows(where[0]), part(k, where[1])
        sums[d][c, rows, at] = (sums[d][c, rows, at].astype(F32) + rs[d, k, i].astype(F32)).astype(BF16)

    def reduce_start(d, k):
        wait_in(sib.at[:, cols(k)], ps_r.at[d, k])
        add_twin(d, k, y_far)
        rs_send(d, k, 0, (y_far, 0), up)
        rs_send(d, k, 3, (y_far, 1), dn)
        add_twin(d, k, y_up)
        rs_send(d, k, 1, (y_up, 1), up)
        add_twin(d, k, y_dn)
        rs_send(d, k, 4, (y_dn, 0), dn)
        add_twin(d, k, y)

    def reduce_middle(d, k):
        add_ring(d, k, (y_up, 0), 0)
        rs_send(d, k, 2, (y_up, 0), up)
        add_ring(d, k, (y_dn, 1), 3)
        rs_send(d, k, 5, (y_dn, 1), dn)

    def reduce_end(d, k):
        rows = block_rows(y)
        for h, ins in enumerate(((4, 2), (1, 5))):
            for i in ins:
                wait_in(rs.at[d, k, i], rs_r.at[d, k, i])
            at = part(k, h)
            sums[d][c, rows, at] = (
                sums[d][c, rows, at].astype(F32) + rs[d, k, ins[0]].astype(F32) + rs[d, k, ins[1]].astype(F32)
            ).astype(BF16)

        def leaving(to):
            return sums[d].at[c, unit_rows(y * block + to * UNIT), cols(k)]

        landing = aback.at[d, unit_rows(e * UNIT), cols(k)]
        pltpu.make_async_copy(leaving(e), landing, bk_r.at[d, k]).start()

        def send(step, carry):
            to = (e + step) % plane
            remote(leaving(to), landing, bk_s.at[d, k], bk_r.at[d, k], dp, to).start()
            return carry

        lax.fori_loop(1, plane, send, 0)

    kept = (mixed, tgrad)
    other_sum = (sibx, sibg)

    def unplace(d, k):
        wait_in(aback.at[d, :, cols(k)], bk_r.at[d, k])
        routed = aback[d, :, cols(k)]
        dims = (((0,), (0,)), ((), ()))
        leave = stage.at[d, pl.ds(0, tokens), cols(k)]
        leave[...] = lax.dot_general(placer_sib, routed, dims, preferred_element_type=F32).astype(BF16)
        remote(leave, other_sum[d].at[:, cols(k)], fn_s.at[d, k], fn_r.at[d, k], twin).start()
        kept[d][:, cols(k)] = lax.dot_general(placer_own, routed, dims, preferred_element_type=F32).astype(BF16)

    def token_rows(d, k):
        wait_in(other_sum[d].at[:, cols(k)], fn_r.at[d, k])
        return kept[d][:, cols(k)].astype(F32) + other_sum[d][:, cols(k)].astype(F32)

    transposed = (((1,), (1,)), ((), ()))
    over_rows = (((0,), (0,)), ((), ()))

    def hidden_back(f):
        def step(t, carry):
            rows = tile(t)
            back = lax.dot_general(G[f, rows, :], wout[f], transposed, preferred_element_type=F32)
            H[f, rows, :] = (back * S[f, rows, :].astype(F32)).astype(BF16)
            return carry

        lax.fori_loop(0, 2, step, 0)

    def token_back(f, k):
        def step(t, carry):
            rows = tile(t)
            G[f, rows, cols(k)] = lax.dot_general(
                H[f, rows, :], win[f, cols(k), :], transposed, preferred_element_type=F32
            ).astype(BF16)
            return carry

        lax.fori_loop(0, 2, step, 0)

    def out_tiles(f):
        def step(n, carry):
            at = pl.ds(pl.multiple_of(n * quarter, quarter), quarter)
            Pf[o, pl.ds(pl.multiple_of(f * hidden_width, hidden_width), hidden_width), at] = lax.dot_general(
                H[f], G[f, :, at], over_rows, preferred_element_type=F32
            ).astype(BF16)
            return carry

        lax.fori_loop(0, CHUNKS, step, 0)

    def in_weights_spot(f, m):
        return (
            o,
            pl.ds(pl.multiple_of(f * quarter, quarter), quarter),
            pl.ds(pl.multiple_of(m * hidden_width, hidden_width), hidden_width),
        )

    def in_copy(f, m):
        return pltpu.make_async_copy(
            Pf.at[in_weights_spot(f, m)], dwin_h.at[f, pl.ds(m * quarter, quarter)], out_s.at[2 + CHUNKS * f + m]
        )

    def in_tiles(f):
        def step(m, carry):
            at = pl.ds(pl.multiple_of(m * quarter, quarter), quarter)
            Pf[in_weights_spot(f, m)] = lax.dot_general(
                X[f, :, at], H[f], over_rows, preferred_element_type=F32
            ).astype(BF16)
            return carry

        lax.fori_loop(0, CHUNKS, step, 0)
        for m in range(CHUNKS):
            in_copy(f, m).start()

    swap[1].wait_recv()
    place(0)
    scatter(0)
    place(1)
    send_own(0)
    scatter(1)
    swap[2].wait_recv()
    place(2)
    place(3)
    send_own(1)
    scatter(2)
    forward_on(0)
    scatter(3)
    take_rest(0)
    place(4)
    place(5)
    send_own(2)
    forward_on(1)
    take_rest(1)
    scatter(4)
    send_own(3)
    forward_on(2)
    take_rest(2)
    scatter(5)
    place(6)
    place(7)
    send_own(4)
    scatter(6)
    forward_on(3)
    take_rest(3)
    send_own(5)
    scatter(7)
    load_in.wait()
    load_out.wait()
    wait_twin(0)
    send_own(6)
    forward(o, 0)
    forward_on(4)
    send_own(7)
    take_rest(4)
    forward(o, 1)
    for k in range(CHUNKS):
        partial_to_twin(0, k)
    forward_on(5)
    take_rest(5)
    forward_on(6)
    forward(c, 0)
    take_rest(6)
    forward_on(7)
    forward(c, 1)

    reduce_start(0, 0)
    reduce_start(0, 1)
    take_rest(7)
    wait_partial_sends(0)
    wait_twin(1)
    out_tiles(o)
    reduce_middle(0, 0)
    out_tiles(c)
    out_copies = [
        pltpu.make_async_copy(Pf.at[o, pl.ds(f * hidden_width, hidden_width)], dwout_h.at[f], out_s.at[f])
        for f in range(2)
    ]
    for copy in out_copies:
        copy.start()
    reduce_start(0, 2)
    reduce_middle(0, 1)
    hidden_back(o)
    reduce_start(0, 3)
    pl.semaphore_signal(credit, inc=1, device_id=(twin, e), device_id_type=MESH)
    reduce_end(0, 0)
    reduce_middle(0, 2)
    hidden_back(c)
    wait_gather_sends(1)
    pl.semaphore_wait(credit, 1)
    token_back(o, 0)
    partial_to_twin(1, 0)
    token_back(c, 0)
    token_back(o, 1)
    partial_to_twin(1, 1)
    token_back(c, 1)
    reduce_end(0, 1)
    reduce_middle(0, 3)
    reduce_start(1, 0)
    token_back(o, 2)
    partial_to_twin(1, 2)
    token_back(c, 2)
    token_back(o, 3)
    partial_to_twin(1, 3)
    token_back(c, 3)
    reduce_start(1, 1)
    reduce_end(0, 2)
    reduce_middle(1, 0)
    reduce_end(0, 3)

    sent_rows = UNIT * (plane - 1)
    for a in range(2):
        for k in range(CHUNKS):
            wait_out(stage.at[a, pl.ds(0, sent_rows), cols(k)], a2a_s.at[a, k])
    for copy in swap:
        copy.wait_send()
    for copy in out_copies:
        copy.wait()
    unplace(0, 0)
    unplace(0, 1)
    reduce_start(1, 2)
    reduce_middle(1, 1)
    in_tiles(0)
    reduce_start(1, 3)
    reduce_end(1, 0)
    reduce_middle(1, 2)
    in_tiles(1)
    unplace(0, 2)
    unplace(0, 3)
    reduce_end(1, 1)
    reduce_middle(1, 3)
    unplace(1, 0)
    gate_total = jnp.zeros((tokens, 1), F32)
    for k in range(CHUNKS):
        out_rows = token_rows(0, k)
        gate_total += jnp.sum(cot[:, cols(k)].astype(F32) * out_rows, 1, keepdims=True)
        mixed[:, cols(k)] = (gate_col * out_rows).astype(BF16)
    ggrad[...] = jnp.sum(jnp.where(diagonal, gate_total, 0.0), 0, keepdims=True)
    reduce_end(1, 2)
    unplace(1, 1)
    reduce_end(1, 3)
    unplace(1, 2)
    unplace(1, 3)
    for k in range(CHUNKS):
        tgrad[:, cols(k)] = token_rows(1, k).astype(BF16)

    wait_gather_sends(0)
    wait_partial_sends(1)
    for f in range(2):
        for m in range(CHUNKS):
            in_copy(f, m).wait()
    for d in range(2):
        for k in range(CHUNKS):
            for i in range(6):
                wait_out(rs.at[d, k, i], rs_s.at[d, k, i])
            wait_out(aback.at[d, pl.ds(0, sent_rows), cols(k)], bk_s.at[d, k])
            wait_out(stage.at[d, pl.ds(0, tokens), cols(k)], fn_s.at[d, k])


def hand_over_kernel(*refs):
    sources, targets, held, sems_in, sems_out = refs[:5], refs[5:10], refs[10:15], refs[15], refs[16]
    pieces = []
    for source, target, mid in zip(sources, targets, held):
        if len(source.shape) == 3:
            half = source.shape[1] // 2
            for f in range(source.shape[0]):
                for n in range(2):
                    at = (f, pl.ds(n * half, half))
                    pieces.append((source.at[at], mid.at[at], target.at[at]))
        else:
            pieces.append((source, mid, target))
    ins = [pltpu.make_async_copy(s, m, sems_in.at[n]) for n, (s, m, t) in enumerate(pieces)]
    outs = [pltpu.make_async_copy(m, t, sems_out.at[n]) for n, (s, m, t) in enumerate(pieces)]
    for copy in ins:
        copy.start()
    for arrived, leaving in zip(ins, outs):
        arrived.wait()
        leaving.start()
    for copy in outs:
        copy.wait()


def local(tokens, expert_ids, gate_weights, in_weights, out_weights, cotangent):
    plane = lax.axis_size("expert")
    count, features = tokens.shape
    hidden_width = in_weights.shape[2]
    block = UNIT * plane
    rows_all = NY * block
    vmem = pl.BlockSpec(memory_space=pltpu.VMEM)
    hbm = pl.BlockSpec(memory_space=pl.ANY)
    dma = pltpu.SemaphoreType.DMA
    shapes = (
        jax.ShapeDtypeStruct((count, features), BF16),
        jax.ShapeDtypeStruct((1, count), F32),
        jax.ShapeDtypeStruct((count, features), BF16),
        jax.ShapeDtypeStruct(in_weights.shape, BF16),
        jax.ShapeDtypeStruct(out_weights.shape, BF16),
    )
    results = pl.pallas_call(
        functools.partial(layer_kernel, plane),
        out_shape=shapes,
        in_specs=[vmem, vmem, vmem, vmem, hbm, hbm],
        out_specs=(vmem, vmem, vmem, hbm, hbm),
        scratch_shapes=[
            pltpu.VMEM((2, 2, rows_all, features), BF16),
            pltpu.VMEM(in_weights.shape, BF16),
            pltpu.VMEM(out_weights.shape, BF16),
            pltpu.VMEM((2, rows_all, hidden_width), BF16),
            pltpu.VMEM((2, rows_all, hidden_width), BF16),
            pltpu.VMEM((2, rows_all, features), BF16),
            pltpu.VMEM((rows_all, features), BF16),
            pltpu.VMEM((2, CHUNKS, 6, block, features // CHUNKS // 2), BF16),
            pltpu.VMEM((2, block, features), BF16),
            pltpu.VMEM((2, block, features), BF16),
            pltpu.VMEM((count, features), BF16),
            pltpu.VMEM((count, features), BF16),
            pltpu.VMEM((count, features), BF16),
            pltpu.VMEM((1, count), jnp.int32),
            dma((3,)), dma((3,)), dma((2,)),
            dma((2, CHUNKS)), dma((2, CHUNKS)),
            dma((2, CHUNKS, 6)), dma((2, CHUNKS, 6)),
            dma((2, CHUNKS, 8)), dma((2, CHUNKS, 8)),
            dma((2, CHUNKS)), dma((2, CHUNKS)),
            dma((2, CHUNKS, 6)), dma((2, CHUNKS, 6)),
            dma((2, CHUNKS)), dma((2, CHUNKS)),
            dma((2, CHUNKS)), dma((2, CHUNKS)),
            dma((2 + 2 * CHUNKS,)),
            pltpu.SemaphoreType.REGULAR,
        ],
        compiler_params=pltpu.CompilerParams(
            collective_id=0, has_side_effects=True, vmem_limit_bytes=60 * 1024 * 1024
        ),
    )(
        tokens, cotangent, gate_weights.reshape(1, count), expert_ids.reshape(1, count), in_weights, out_weights,
    )
    mixed, gate_grad, token_grad, in_grad, out_grad = pl.pallas_call(
        hand_over_kernel,
        out_shape=shapes,
        in_specs=[pl.BlockSpec(memory_space=pltpu.HBM)] * 5,
        out_specs=(pl.BlockSpec(memory_space=pltpu.HBM),) * 5,
        scratch_shapes=[pltpu.VMEM(shape.shape, shape.dtype) for shape in shapes] + [dma((11,)), dma((11,))],
        compiler_params=pltpu.CompilerParams(vmem_limit_bytes=60 * 1024 * 1024),
    )(*results)
    return mixed, gate_grad.reshape(count), token_grad, in_grad, out_grad


def solution(mesh):
    in_specs = (
        P(("dp", "expert"), None),
        P(("dp", "expert")),
        P(("dp", "expert")),
        P("expert", None, "dp"),
        P("expert", "dp", None),
        P(("dp", "expert"), None),
    )
    out_specs = (
        P(("dp", "expert"), None),
        P(("dp", "expert")),
        P(("dp", "expert"), None),
        P("expert", None, "dp"),
        P("expert", "dp", None),
    )
    return jax.shard_map(local, mesh=mesh, in_specs=in_specs, out_specs=out_specs, check_vma=False)
```

time: 346 us -> 185 us (0.53); the launches traced: 341 us -> 185 us
  Pallas kernels: 0 us -> 184 us
  waiting for transfers between devices: 163 us -> 0 us
  matrix products: 66.6 us -> 0 us
  blocking collectives: 56.7 us -> 0 us
  starting transfers between devices: 27.2 us -> 0 us
  between operations: 14.4 us -> 0.8 us
  other arithmetic: 9.8 us -> 0 us
  local copies, waits for them, and re-layouts: 3.89 us -> 0 us
    pallas_call x0 -> x2, Pallas kernels: none -> 184 us  [the longest x1 177 us: local(): pl.pallas_call(functools.partial(layer_kernel, plane), out_shape=shapes,...]
    reduce_scatter x4 -> x0, waiting for transfers between devices: 93.4 us -> none  [route_back(): lax.psum_scatter(term.astype(jnp.bfloat16), 'dp', scatter_dimension=0, ti...]
    dot_general x16 -> x0, matrix products: 66.6 us -> none  [the longest x12 62.8 us: local(): lax.dot_general(a, b, (dims, ((), ())), preferred_element_type=jnp.float32)]
    all_gather x4 -> x0, waiting for transfers between devices: 61.9 us -> none  [route(): lax.all_gather(swapped.reshape(ex_count * capacity, features), 'dp', axis...]
    all_to_all x4 -> x0, blocking collectives: 56.7 us -> none  [route(): lax.all_to_all(by_expert[:, f], 'expert', split_axis=0, concat_axis=0, ti...]
    all_to_all x4 -> x0, starting transfers between devices: 26.7 us -> none  [route_back(): lax.all_to_all(summed.reshape(ex_count, capacity, term.shape[1]), 'expert...]
    another operation x5 -> x0, other arithmetic: 7.52 us -> none  [the longest x1 4.77 us: local(): jnp.stack(in_grads)]
    all_to_all x4 -> x0, waiting for transfers between devices: 7.3 us -> none  [route_back(): lax.all_to_all(summed.reshape(ex_count, capacity, term.shape[1]), 'expert...]
  transfers between devices with their start and end apart: 12 -> 0, of which waited for: 8 -> 0; matrix products, arithmetic and copies ran while one was open for 21% -> 0% of each run, Pallas kernels for 0% -> 0%
where the time goes in v3:
time: 185 us
  Pallas kernels  184 us (99%)
    pallas_call x1, Pallas kernels, local(): pl.pallas_call(functools.partial(layer_kernel, plane), out_shape=shapes,...  177 us
    pallas_call x1, Pallas kernels, local(): pl.pallas_call(hand_over_kernel, out_shape=shapes, in_specs=[pl.BlockSpec...  7.43 us

profile of v3, /device:TPU:1, one launch (start us, length us, event | category | flops | bytes accessed | tf_op | source)
XLA Modules:
  0.0 185.0 jit_solution(13620279772216130585)
XLA Ops:
  0.6 176.8 %shard_map.101 = (bf16[128,2048]{1,0:T(8,128)(2,1)}, f32[1,128]{1,0:T(1,128)}, bf16[128,2048]{1,0:T(8,128)(2,1)}, bf16[2,2048,512]{2,1,0:T(8,128)(2,1)}, bf16[2,512,2048]{2,1,0:T(8,128)(2,1)}) custom-call(bf16[128,2048]{1,0:T(8,128)(2,1)} %tok.1, bf16[128,2048]{1,0:T(8,128)(2,1)} %cot.1, f32[1,128]{1,0:T(1,128)} %bitcast.3, s32[1,128]{1,0:T(1,128)} %bitcast.4, ...), custom_call_target="tpu_custom_call" | custom-call | tf_op jit(solution)/shard_map/pallas_call | solution.py:522
  177.4 7.4 %shard_map.102 = (bf16[128,2048]{1,0:T(8,128)(2,1)}, f32[1,128]{1,0:T(1,128)}, bf16[128,2048]{1,0:T(8,128)(2,1)}, bf16[2,2048,512]{2,1,0:T(8,128)(2,1)}, bf16[2,512,2048]{2,1,0:T(8,128)(2,1)}) custom-call(bf16[128,2048]{1,0:T(8,128)(2,1)} %get-tuple-element.15.refs_0_, f32[1,128]{1,0:T(1,128)} %get-tuple-element.16.refs_1_, ...), custom_call_target="tpu_custom_call" | custom-call | tf_op jit(solution)/shard_map/pallas_call | solution.py:559

commit v4 on v3

--- a/solution.py
+++ b/solution.py
@@ -14,6 +14,7 @@
 UNIT = 2 * CAP
 NY = 4
 CHUNKS = 4
+LAST = CHUNKS - 1
 BF16, F32 = jnp.bfloat16, jnp.float32
 
 
@@ -21,9 +22,9 @@
     plane,
     tok, cot, gate, ids, win_h, wout_h,
     mixed, ggrad, tgrad, dwin_h, dwout_h,
-    XG, win, wout, S, H, Pf, sib, rs, stage, aback, gown, sibx, sibg, sibids,
+    XG, win, wout, S, H, Pf, sib, rs, rs_raw, stage, aback, aback_all, gown, sibx, sibg, all_ids, placers,
     swap_s, swap_r, w_s, a2a_s, a2a_r, ag_s, ag_r, sb_s, sb_r, ps_s, ps_r, rs_s, rs_r,
-    bk_s, bk_r, fn_s, fn_r, out_s, credit,
+    bk_s, bk_r, fn_s, fn_r, out_s, ids_s, ids_r, raw_s, raw_r, rt_s, rt_r, ab_s, ab_r, bb_s, bb_r, ft_s, ft_r, credit,
 ):
     tokens, features = tok.shape
     block = UNIT * plane
@@ -75,8 +76,11 @@
         pl.semaphore_signal(barrier, inc=1, device_id=(dp, (e + k) % plane), device_id_type=MESH)
         return carry
 
-    for other in (twin, up, dn):
-        pl.semaphore_signal(barrier, inc=1, device_id=(other, e), device_id_type=MESH)
+    def greet_dp(k, carry):
+        pl.semaphore_signal(barrier, inc=1, device_id=((dp + k) % (2 * NY), e), device_id_type=MESH)
+        return carry
+
+    lax.fori_loop(1, 2 * NY, greet_dp, 0)
     lax.fori_loop(1, plane, greet, 0)
 
     diagonal = lax.broadcasted_iota(jnp.int32, (tokens, tokens), 0) == lax.broadcasted_iota(
@@ -99,29 +103,105 @@
         target = jnp.where((id_row & 1) == c, target, -1)
         return (lax.broadcasted_iota(jnp.int32, (block, tokens), 0) == target).astype(F32).astype(BF16)
 
-    placer_own = placer_of(ids[...], c)
-    pl.semaphore_wait(barrier, plane + 2)
-
+    placers[0, y] = placer_of(ids[...], c)
+    pl.semaphore_wait(barrier, plane - 1 + 2 * NY - 1)
+
+    for k in range(1, 2 * NY):
+        remote(ids, all_ids.at[dp], ids_s.at[k], ids_r.at[k], (dp + k) % (2 * NY)).start()
     swap = [
-        remote(ids, sibids, swap_s.at[0], swap_r.at[0], twin),
-        remote(tok, sibx, swap_s.at[1], swap_r.at[1], twin),
-        remote(gown, sibg, swap_s.at[2], swap_r.at[2], twin),
+        remote(tok, sibx, swap_s.at[0], swap_r.at[0], twin),
+        remote(gown, sibg, swap_s.at[1], swap_r.at[1], twin),
     ]
-    for copy in swap:
-        copy.start()
-    load_in.start()
-    load_out.start()
-    swap[0].wait_recv()
-    placer_sib = placer_of(sibids[...], o)
 
     own_src = (tok, gown)
     sib_src = (sibx, sibg)
     chunks = [(a, k) for a in range(2) for k in range(CHUNKS)]
 
+    blocks_y = (y, y_up, y_dn, y_far)
+
+    def raw_rows(core, yb):
+        return pl.ds(pl.multiple_of((core * NY + yb) * tokens, tokens), tokens)
+
+    def raw_at(a, core, yb, h):
+        return Pf.at[a, raw_rows(core, yb), pl.ds(h * eighth, eighth)]
+
+    def raw_own(a):
+        for h in range(2):
+            for n, to in ((h, up), (2 + h, dn)):
+                remote(
+                    own_src[a].at[:, part(LAST, h)], raw_at(a, c, y, h), raw_s.at[a, n], raw_r.at[a, n], to
+                ).start()
+
+    def raw_to_twin(a, i):
+        yb, h = raw_pieces[i]
+        ref = raw_at(a, c, yb, h)
+        remote(ref, ref, rt_s.at[a, i], rt_r.at[a, i], twin).start()
+
+    raw_pieces = ((y_dn, 0), (y_dn, 1), (y_up, 0), (y_up, 1), (y_far, 0), (y_far, 1))
+
+    def raw_forward(a):
+        for i, n, to in ((0, 4, up), (3, 5, dn)):
+            ref = raw_at(a, c, *raw_pieces[i])
+            wait_in(ref, raw_r.at[a, i])
+            remote(ref, ref, raw_s.at[a, n], raw_r.at[a, n], to).start()
+            raw_to_twin(a, i)
+
+    def raw_rest(a):
+        for i in (1, 2, 4, 5):
+            wait_in(raw_at(a, c, *raw_pieces[i]), raw_r.at[a, i])
+            raw_to_twin(a, i)
+
+    def raw_wait_twin(a):
+        for i in range(6):
+            wait_in(raw_at(a, o, *raw_pieces[i]), rt_r.at[a, i])
+
+    def raw_wait_sends(a):
+        for i in range(6):
+            wait_out(raw_at(a, c, y, 0), raw_s.at[a, i])
+            wait_out(raw_at(a, c, y, 0), rt_s.at[a, i])
+
+    def wide_stage(a, yb):
+        if a == 0:
+            return Pf.at[0, block_rows(yb), pl.ds(quarter, quarter)]
+        return sib.at[block_rows(yb), pl.ds(0, quarter)]
+
+    def wide_place(a):
+        for j, yb in enumerate(blocks_y):
+            if j == 0:
+                mine, theirs = own_src[a][:, cols(LAST)], sib_src[a][:, cols(LAST)]
+            else:
+                mine = Pf[a, raw_rows(c, yb), pl.ds(0, quarter)]
+                theirs = Pf[a, raw_rows(o, yb), pl.ds(0, quarter)]
+            placed = jnp.dot(placers[0, yb], mine, preferred_element_type=F32)
+            placed += jnp.dot(placers[1, yb], theirs, preferred_element_type=F32)
+            wide_stage(a, yb)[...] = placed.astype(BF16)
+
+    def wide_scatter(a, j):
+        yb = blocks_y[j]
+        landing = XG.at[a, c, unit_rows(yb * block + e * UNIT), cols(LAST)]
+        source = wide_stage(a, yb)
+        pltpu.make_async_copy(source.at[unit_rows(e * UNIT)], landing, ab_r.at[a, j]).start()
+
+        def send(step, carry):
+            to = (e + step) % plane
+            remote(source.at[unit_rows(to * UNIT)], landing, ab_s.at[a, j], ab_r.at[a, j], dp, to).start()
+            return carry
+
+        lax.fori_loop(1, plane, send, 0)
+
+    def wide_wait_sends(a):
+        for j in range(NY):
+            wait_out(wide_stage(a, y).at[pl.ds(0, UNIT * (plane - 1))], ab_s.at[a, j])
+
+    def wide_arrived(a, j):
+        ref = XG.at[a, c, block_rows(blocks_y[j]), cols(LAST)]
+        wait_in(ref, ab_r.at[a, j])
+        remote(ref, ref, sb_s.at[a, LAST, j], sb_r.at[a, LAST, j], twin).start()
+
     def place(q):
         a, k = chunks[q]
-        placed = jnp.dot(placer_own, own_src[a][:, cols(k)], preferred_element_type=F32)
-        placed += jnp.dot(placer_sib, sib_src[a][:, cols(k)], preferred_element_type=F32)
+        placed = jnp.dot(placers[0, y], own_src[a][:, cols(k)], preferred_element_type=F32)
+        placed += jnp.dot(placers[1, y], sib_src[a][:, cols(k)], preferred_element_type=F32)
         stage[a, :, cols(k)] = placed.astype(BF16)
 
     def scatter(q):
@@ -174,13 +254,17 @@
             to_twin(q, i, ring_pieces[i])
 
     def wait_twin(a):
-        for k in range(CHUNKS):
+        for j in range(NY):
+            wait_in(XG.at[a, o, block_rows(blocks_y[j]), cols(LAST)], sb_r.at[a, LAST, j])
+        for k in range(LAST):
             q = a * CHUNKS + k
             for n, where in enumerate(ring_pieces + ((y, 0), (y, 1))):
                 wait_in(piece(q, o, where), sb_r.at[a, k, n])
 
     def wait_gather_sends(a):
-        for k in range(CHUNKS):
+        for j in range(NY):
+            wait_out(XG.at[a, c, block_rows(y), cols(LAST)], sb_s.at[a, LAST, j])
+        for k in range(LAST):
             q = a * CHUNKS + k
             for n in range(6):
                 wait_out(piece(q, c, (y, 0)), ag_s.at[a, k, n])
@@ -272,11 +356,79 @@
         routed = aback[d, :, cols(k)]
         dims = (((0,), (0,)), ((), ()))
         leave = stage.at[d, pl.ds(0, tokens), cols(k)]
-        leave[...] = lax.dot_general(placer_sib, routed, dims, preferred_element_type=F32).astype(BF16)
+        leave[...] = lax.dot_general(placers[1, y], routed, dims, preferred_element_type=F32).astype(BF16)
         remote(leave, other_sum[d].at[:, cols(k)], fn_s.at[d, k], fn_r.at[d, k], twin).start()
-        kept[d][:, cols(k)] = lax.dot_general(placer_own, routed, dims, preferred_element_type=F32).astype(BF16)
+        kept[d][:, cols(k)] = lax.dot_general(placers[0, y], routed, dims, preferred_element_type=F32).astype(BF16)
+
+    def wide_leave(d):
+        wait_in(sib.at[:, cols(LAST)], ps_r.at[d, LAST])
+        for j, yb in enumerate(blocks_y):
+            add_twin(d, LAST, yb)
+            landing = aback_all.at[d, yb, unit_rows(e * UNIT)]
+            source = sums[d].at[c, block_rows(yb), cols(LAST)]
+            pltpu.make_async_copy(source.at[unit_rows(e * UNIT)], landing, bb_r.at[d, j]).start()
+
+            def send(step, carry, j=j, landing=landing, source=source):
+                to = (e + step) % plane
+                remote(source.at[unit_rows(to * UNIT)], landing, bb_s.at[d, j], bb_r.at[d, j], dp, to).start()
+                return carry
+
+            lax.fori_loop(1, plane, send, 0)
+
+    def raw_in(d, yb):
+        return S.at[d, pl.ds(pl.multiple_of(yb * tokens, tokens), tokens), pl.ds(0, quarter)]
+
+    def wide_unplace(d):
+        dims = (((0,), (0,)), ((), ()))
+        for j, yb in enumerate(blocks_y):
+            wait_in(aback_all.at[d, yb], bb_r.at[d, j])
+            routed = aback_all[d, yb]
+            mine = lax.dot_general(placers[0, yb], routed, dims, preferred_element_type=F32).astype(BF16)
+            theirs = lax.dot_general(placers[1, yb], routed, dims, preferred_element_type=F32).astype(BF16)
+            aback_all[d, yb, pl.ds(0, tokens)] = mine
+            leave = aback_all.at[d, yb, pl.ds(tokens, tokens)]
+            leave[...] = theirs
+            remote(leave, raw_in(d, yb), ft_s.at[d, j], ft_r.at[d, j], twin).start()
+
+    def raw_total(d, where):
+        return aback_all.at[d, where[0], pl.ds(0, tokens), pl.ds(where[1] * eighth, eighth)]
+
+    def raw_send(d, i, where, to):
+        remote(raw_total(d, where), rs_raw.at[d, i], rs_s.at[d, LAST, i], rs_r.at[d, LAST, i], to).start()
+
+    def raw_add(d, where, i):
+        wait_in(rs_raw.at[d, i], rs_r.at[d, LAST, i])
+        ref = raw_total(d, where)
+        ref[...] = (ref[...].astype(F32) + rs_raw[d, i].astype(F32)).astype(BF16)
+
+    def raw_sum_start(d):
+        for j in (3, 1, 2, 0):
+            yb = blocks_y[j]
+            wait_in(raw_in(d, yb), ft_r.at[d, j])
+            own = aback_all.at[d, yb, pl.ds(0, tokens)]
+            own[...] = (own[...].astype(F32) + raw_in(d, yb)[...].astype(F32)).astype(BF16)
+        raw_send(d, 0, (y_far, 0), up)
+        raw_send(d, 3, (y_far, 1), dn)
+        raw_send(d, 1, (y_up, 1), up)
+        raw_send(d, 4, (y_dn, 0), dn)
+
+    def raw_sum_middle(d):
+        raw_add(d, (y_up, 0), 0)
+        raw_send(d, 2, (y_up, 0), up)
+        raw_add(d, (y_dn, 1), 3)
+        raw_send(d, 5, (y_dn, 1), dn)
+
+    def raw_sum_end(d):
+        for h, ins in enumerate(((4, 2), (1, 5))):
+            for i in ins:
+                wait_in(rs_raw.at[d, i], rs_r.at[d, LAST, i])
+            kept[d][:, part(LAST, h)] = (
+                raw_total(d, (y, h))[...].astype(F32) + rs_raw[d, ins[0]].astype(F32) + rs_raw[d, ins[1]].astype(F32)
+            ).astype(BF16)
 
     def token_rows(d, k):
+        if k == LAST:
+            return kept[d][:, cols(k)].astype(F32)
         wait_in(other_sum[d].at[:, cols(k)], fn_r.at[d, k])
         return kept[d][:, cols(k)].astype(F32) + other_sum[d][:, cols(k)].astype(F32)
 
@@ -336,60 +488,94 @@
         for m in range(CHUNKS):
             in_copy(f, m).start()
 
-    swap[1].wait_recv()
+    swap[0].start()
+    raw_own(0)
+    swap[1].start()
+    raw_own(1)
+    load_in.start()
+    load_out.start()
+
+    for k in range(1, 2 * NY):
+        wait_in(all_ids.at[(dp + 2 * NY - k) % (2 * NY)], ids_r.at[k])
+    placers[1, y] = placer_of(all_ids[twin], o)
+    swap[0].wait_recv()
     place(0)
     scatter(0)
+    for yb in (y_dn, y_up, y_far):
+        placers[0, yb] = placer_of(all_ids[yb * 2 + c], c)
+        placers[1, yb] = placer_of(all_ids[yb * 2 + o], o)
+    raw_forward(0)
     place(1)
     send_own(0)
     scatter(1)
-    swap[2].wait_recv()
+    raw_rest(0)
+    raw_forward(1)
     place(2)
-    place(3)
     send_own(1)
     scatter(2)
     forward_on(0)
-    scatter(3)
-    take_rest(0)
+    raw_wait_twin(0)
+    wide_place(0)
+    wide_scatter(0, 0)
+    wide_scatter(0, 1)
+    swap[1].wait_recv()
     place(4)
     place(5)
+    place(6)
+    take_rest(0)
     send_own(2)
+    wide_scatter(0, 2)
+    wide_scatter(0, 3)
     forward_on(1)
+    raw_rest(1)
+    raw_wait_twin(1)
+    wide_place(1)
+    scatter(4)
     take_rest(1)
-    scatter(4)
-    send_own(3)
     forward_on(2)
+    wide_arrived(0, 0)
+    wide_arrived(0, 1)
+    send_own(4)
+    scatter(5)
+    wide_scatter(1, 0)
     take_rest(2)
-    scatter(5)
-    place(6)
-    place(7)
-    send_own(4)
+    wide_arrived(0, 2)
+    wide_arrived(0, 3)
     scatter(6)
-    forward_on(3)
-    take_rest(3)
+    wide_scatter(1, 1)
     send_own(5)
-    scatter(7)
+    wide_scatter(1, 2)
+    wide_scatter(1, 3)
+    raw_wait_sends(0)
+    raw_wait_sends(1)
+    wide_wait_sends(0)
     load_in.wait()
     load_out.wait()
     wait_twin(0)
-    send_own(6)
     forward(o, 0)
     forward_on(4)
-    send_own(7)
+    send_own(6)
     take_rest(4)
+    forward_on(5)
+    wide_arrived(1, 0)
+    wide_arrived(1, 1)
     forward(o, 1)
-    for k in range(CHUNKS):
+    wide_arrived(1, 2)
+    wide_arrived(1, 3)
+    wide_wait_sends(1)
+    pl.semaphore_signal(credit, inc=1, device_id=(twin, e), device_id_type=MESH)
+    pl.semaphore_wait(credit, 1)
+    for k in (LAST, 0, 1, 2):
         partial_to_twin(0, k)
-    forward_on(5)
     take_rest(5)
     forward_on(6)
     forward(c, 0)
     take_rest(6)
-    forward_on(7)
     forward(c, 1)
 
     reduce_start(0, 0)
+    wide_leave(0)
     reduce_start(0, 1)
-    take_rest(7)
     wait_partial_sends(0)
     wait_twin(1)
     out_tiles(o)
@@ -402,78 +588,87 @@
     for copy in out_copies:
         copy.start()
     reduce_start(0, 2)
+    pl.semaphore_signal(credit, inc=1, device_id=(twin, e), device_id_type=MESH)
     reduce_middle(0, 1)
     hidden_back(o)
-    reduce_start(0, 3)
-    pl.semaphore_signal(credit, inc=1, device_id=(twin, e), device_id_type=MESH)
     reduce_end(0, 0)
-    reduce_middle(0, 2)
     hidden_back(c)
     wait_gather_sends(1)
     pl.semaphore_wait(credit, 1)
+    token_back(o, LAST)
+    partial_to_twin(1, LAST)
+    token_back(c, LAST)
+    reduce_middle(0, 2)
     token_back(o, 0)
     partial_to_twin(1, 0)
     token_back(c, 0)
+    wide_leave(1)
+    wide_unplace(0)
+    reduce_start(1, 0)
     token_back(o, 1)
     partial_to_twin(1, 1)
     token_back(c, 1)
     reduce_end(0, 1)
-    reduce_middle(0, 3)
-    reduce_start(1, 0)
+    raw_sum_start(0)
     token_back(o, 2)
     partial_to_twin(1, 2)
     token_back(c, 2)
-    token_back(o, 3)
-    partial_to_twin(1, 3)
-    token_back(c, 3)
     reduce_start(1, 1)
     reduce_end(0, 2)
     reduce_middle(1, 0)
-    reduce_end(0, 3)
+    raw_sum_middle(0)
+    wide_unplace(1)
+    raw_sum_start(1)
 
     sent_rows = UNIT * (plane - 1)
     for a in range(2):
-        for k in range(CHUNKS):
+        for k in range(LAST):
             wait_out(stage.at[a, pl.ds(0, sent_rows), cols(k)], a2a_s.at[a, k])
     for copy in swap:
         copy.wait_send()
     for copy in out_copies:
         copy.wait()
     unplace(0, 0)
-    unplace(0, 1)
     reduce_start(1, 2)
     reduce_middle(1, 1)
+    raw_sum_middle(1)
     in_tiles(0)
-    reduce_start(1, 3)
     reduce_end(1, 0)
+    unplace(0, 1)
     reduce_middle(1, 2)
+    raw_sum_end(0)
     in_tiles(1)
+    reduce_end(1, 1)
     unplace(0, 2)
-    unplace(0, 3)
-    reduce_end(1, 1)
-    reduce_middle(1, 3)
-    unplace(1, 0)
+    raw_sum_end(1)
     gate_total = jnp.zeros((tokens, 1), F32)
     for k in range(CHUNKS):
         out_rows = token_rows(0, k)
         gate_total += jnp.sum(cot[:, cols(k)].astype(F32) * out_rows, 1, keepdims=True)
         mixed[:, cols(k)] = (gate_col * out_rows).astype(BF16)
     ggrad[...] = jnp.sum(jnp.where(diagonal, gate_total, 0.0), 0, keepdims=True)
+    unplace(1, 0)
     reduce_end(1, 2)
     unplace(1, 1)
-    reduce_end(1, 3)
+    tgrad[:, cols(0)] = token_rows(1, 0).astype(BF16)
+    tgrad[:, cols(1)] = token_rows(1, 1).astype(BF16)
     unplace(1, 2)
-    unplace(1, 3)
-    for k in range(CHUNKS):
-        tgrad[:, cols(k)] = token_rows(1, k).astype(BF16)
+    tgrad[:, cols(2)] = token_rows(1, 2).astype(BF16)
 
     wait_gather_sends(0)
     wait_partial_sends(1)
     for f in range(2):
         for m in range(CHUNKS):
             in_copy(f, m).wait()
+    for k in range(1, 2 * NY):
+        wait_out(ids, ids_s.at[k])
     for d in range(2):
-        for k in range(CHUNKS):
+        for i in range(6):
+            wait_out(rs_raw.at[d, i], rs_s.at[d, LAST, i])
+        for j in range(NY):
+            wait_out(aback_all.at[d, y, pl.ds(0, sent_rows)], bb_s.at[d, j])
+            wait_out(raw_in(d, y), ft_s.at[d, j])
+        for k in range(LAST):
             for i in range(6):
                 wait_out(rs.at[d, k, i], rs_s.at[d, k, i])
             wait_out(aback.at[d, pl.ds(0, sent_rows), cols(k)], bk_s.at[d, k])
@@ -509,6 +704,7 @@
     hidden_width = in_weights.shape[2]
     block = UNIT * plane
     rows_all = NY * block
+    quarter = features // CHUNKS
     vmem = pl.BlockSpec(memory_space=pltpu.VMEM)
     hbm = pl.BlockSpec(memory_space=pl.ANY)
     dma = pltpu.SemaphoreType.DMA
@@ -532,14 +728,17 @@
             pltpu.VMEM((2, rows_all, hidden_width), BF16),
             pltpu.VMEM((2, rows_all, features), BF16),
             pltpu.VMEM((rows_all, features), BF16),
-            pltpu.VMEM((2, CHUNKS, 6, block, features // CHUNKS // 2), BF16),
-            pltpu.VMEM((2, block, features), BF16),
-            pltpu.VMEM((2, block, features), BF16),
+            pltpu.VMEM((2, LAST, 6, block, quarter // 2), BF16),
+            pltpu.VMEM((2, 6, count, quarter // 2), BF16),
+            pltpu.VMEM((2, block, LAST * quarter), BF16),
+            pltpu.VMEM((2, block, LAST * quarter), BF16),
+            pltpu.VMEM((2, NY, block, quarter), BF16),
             pltpu.VMEM((count, features), BF16),
             pltpu.VMEM((count, features), BF16),
             pltpu.VMEM((count, features), BF16),
-            pltpu.VMEM((1, count), jnp.int32),
-            dma((3,)), dma((3,)), dma((2,)),
+            pltpu.VMEM((2 * NY, 1, count), jnp.int32),
+            pltpu.VMEM((2, NY, block, count), BF16),
+            dma((2,)), dma((2,)), dma((2,)),
             dma((2, CHUNKS)), dma((2, CHUNKS)),
             dma((2, CHUNKS, 6)), dma((2, CHUNKS, 6)),
             dma((2, CHUNKS, 8)), dma((2, CHUNKS, 8)),
@@ -548,6 +747,12 @@
             dma((2, CHUNKS)), dma((2, CHUNKS)),
             dma((2, CHUNKS)), dma((2, CHUNKS)),
             dma((2 + 2 * CHUNKS,)),
+            dma((2 * NY,)), dma((2 * NY,)),
+            dma((2, 6)), dma((2, 6)),
+            dma((2, 6)), dma((2, 6)),
+            dma((2, NY)), dma((2, NY)),
+            dma((2, NY)), dma((2, NY)),
+            dma((2, NY)), dma((2, NY)),
             pltpu.SemaphoreType.REGULAR,
         ],
         compiler_params=pltpu.CompilerParams(

time: 185 us -> 163 us (0.88)
  Pallas kernels: 184 us -> 162 us
    pallas_call x1, Pallas kernels: 177 us -> 155 us  [local(): pl.pallas_call(functools.partial(layer_kernel, plane), out_shape=shapes,...]
where the time goes in v4:
time: 163 us
  Pallas kernels  162 us (99%)
    pallas_call x1, Pallas kernels, local(): pl.pallas_call(functools.partial(layer_kernel, plane), out_shape=shapes,...  155 us
    pallas_call x1, Pallas kernels, local(): pl.pallas_call(hand_over_kernel, out_shape=shapes, in_specs=[pl.BlockSpec...  7.43 us

profile of v4, /device:TPU:1, one launch (start us, length us, event | category | flops | bytes accessed | tf_op | source)
XLA Modules:
  0.0 163.1 jit_solution(4710876121915982760)
XLA Ops:
  0.6 154.9 %shard_map.101 = (bf16[128,2048]{1,0:T(8,128)(2,1)}, f32[1,128]{1,0:T(1,128)}, bf16[128,2048]{1,0:T(8,128)(2,1)}, bf16[2,2048,512]{2,1,0:T(8,128)(2,1)}, bf16[2,512,2048]{2,1,0:T(8,128)(2,1)}) custom-call(bf16[128,2048]{1,0:T(8,128)(2,1)} %tok.1, bf16[128,2048]{1,0:T(8,128)(2,1)} %cot.1, f32[1,128]{1,0:T(1,128)} %bitcast.3, s32[1,128]{1,0:T(1,128)} %bitcast.4, ...), custom_call_target="tpu_custom_call" | custom-call | tf_op jit(solution)/shard_map/pallas_call | solution.py:718
  155.5 7.4 %shard_map.102 = (bf16[128,2048]{1,0:T(8,128)(2,1)}, f32[1,128]{1,0:T(1,128)}, bf16[128,2048]{1,0:T(8,128)(2,1)}, bf16[2,2048,512]{2,1,0:T(8,128)(2,1)}, bf16[2,512,2048]{2,1,0:T(8,128)(2,1)}) custom-call(bf16[128,2048]{1,0:T(8,128)(2,1)} %get-tuple-element.15.refs_0_, f32[1,128]{1,0:T(1,128)} %get-tuple-element.16.refs_1_, ...), custom_call_target="tpu_custom_call" | custom-call | tf_op jit(solution)/shard_map/pallas_call | solution.py:764

commit v5 on v4

--- a/solution.py
+++ b/solution.py
@@ -524,24 +524,24 @@
     place(6)
     take_rest(0)
     send_own(2)
+    scatter(4)
     wide_scatter(0, 2)
     wide_scatter(0, 3)
     forward_on(1)
     raw_rest(1)
     raw_wait_twin(1)
     wide_place(1)
-    scatter(4)
+    scatter(5)
     take_rest(1)
     forward_on(2)
     wide_arrived(0, 0)
     wide_arrived(0, 1)
     send_own(4)
-    scatter(5)
+    scatter(6)
     wide_scatter(1, 0)
     take_rest(2)
     wide_arrived(0, 2)
     wide_arrived(0, 3)
-    scatter(6)
     wide_scatter(1, 1)
     send_own(5)
     wide_scatter(1, 2)
@@ -617,8 +617,6 @@
     reduce_end(0, 2)
     reduce_middle(1, 0)
     raw_sum_middle(0)
-    wide_unplace(1)
-    raw_sum_start(1)
 
     sent_rows = UNIT * (plane - 1)
     for a in range(2):
@@ -631,8 +629,9 @@
     unplace(0, 0)
     reduce_start(1, 2)
     reduce_middle(1, 1)
-    raw_sum_middle(1)
     in_tiles(0)
+    wide_unplace(1)
+    raw_sum_start(1)
     reduce_end(1, 0)
     unplace(0, 1)
     reduce_middle(1, 2)
@@ -640,7 +639,7 @@
     in_tiles(1)
     reduce_end(1, 1)
     unplace(0, 2)
-    raw_sum_end(1)
+    raw_sum_middle(1)
     gate_total = jnp.zeros((tokens, 1), F32)
     for k in range(CHUNKS):
         out_rows = token_rows(0, k)
@@ -649,6 +648,7 @@
     ggrad[...] = jnp.sum(jnp.where(diagonal, gate_total, 0.0), 0, keepdims=True)
     unplace(1, 0)
     reduce_end(1, 2)
+    raw_sum_end(1)
     unplace(1, 1)
     tgrad[:, cols(0)] = token_rows(1, 0).astype(BF16)
     tgrad[:, cols(1)] = token_rows(1, 1).astype(BF16)

time: 163 us -> 162 us (level)
  no operation moved by 1% of the time
where the time goes in v5:
time: 162 us
  Pallas kernels  161 us (99%)
    pallas_call x1, Pallas kernels, local(): pl.pallas_call(functools.partial(layer_kernel, plane), out_shape=shapes,...  154 us
    pallas_call x1, Pallas kernels, local(): pl.pallas_call(hand_over_kernel, out_shape=shapes, in_specs=[pl.BlockSpec...  7.43 us

profile of v5, /device:TPU:1, one launch (start us, length us, event | category | flops | bytes accessed | tf_op | source)
XLA Modules:
  0.0 161.8 jit_solution(3899859935742723229)
XLA Ops:
  0.6 153.6 %shard_map.101 = (bf16[128,2048]{1,0:T(8,128)(2,1)}, f32[1,128]{1,0:T(1,128)}, bf16[128,2048]{1,0:T(8,128)(2,1)}, bf16[2,2048,512]{2,1,0:T(8,128)(2,1)}, bf16[2,512,2048]{2,1,0:T(8,128)(2,1)}) custom-call(bf16[128,2048]{1,0:T(8,128)(2,1)} %tok.1, bf16[128,2048]{1,0:T(8,128)(2,1)} %cot.1, f32[1,128]{1,0:T(1,128)} %bitcast.3, s32[1,128]{1,0:T(1,128)} %bitcast.4, ...), custom_call_target="tpu_custom_call" | custom-call | tf_op jit(solution)/shard_map/pallas_call | solution.py:718
  154.2 7.4 %shard_map.102 = (bf16[128,2048]{1,0:T(8,128)(2,1)}, f32[1,128]{1,0:T(1,128)}, bf16[128,2048]{1,0:T(8,128)(2,1)}, bf16[2,2048,512]{2,1,0:T(8,128)(2,1)}, bf16[2,512,2048]{2,1,0:T(8,128)(2,1)}) custom-call(bf16[128,2048]{1,0:T(8,128)(2,1)} %get-tuple-element.15.refs_0_, f32[1,128]{1,0:T(1,128)} %get-tuple-element.16.refs_1_, ...), custom_call_target="tpu_custom_call" | custom-call | tf_op jit(solution)/shard_map/pallas_call | solution.py:764
